TPU v7x, 32 devices: a whole 2x2x4 slice. The times are simulated.
32 devices in a mesh: section: 2 (over core), seq: 4 (over z), head: 4 (over y, x).
Axes of the slice: x: 2, y: 2, z: 4, core: 2. Of those that a mesh axis runs over, the one named last changes fastest.
Arguments:
- inputs: bfloat16 [2, 1024, 1024], P(None, 'seq'), may hold values from -6 to 6
- cotangent: bfloat16 [2, 1024, 1024], P(None, 'seq'), may hold values from -6 to 6
- in_gain: float32 [2, 1024], P('section'), may hold values from 0.5 to 1.5
- w_z: bfloat16 [2, 1024, 2048], P('section', None, 'head'), may hold values from -0.1875 to 0.1875
- w_x: bfloat16 [2, 1024, 2048], P('section', None, 'head'), may hold values from -0.1875 to 0.1875
- w_bc: bfloat16 [2, 1024, 2, 128], P('section', None, None, 'head'), may hold values from -0.046875 to 0.046875
- w_dt: bfloat16 [2, 1024, 32], P('section', None, 'head'), may hold values from -0.1875 to 0.1875
- dt_bias: float32 [2, 32], P('section', 'head'), may hold values from -3 to 0
- a_log: float32 [2, 32], P('section', 'head'), may hold values from -9 to -1
- skip: float32 [2, 32], P('section', 'head'), may hold values from 0.5 to 1.5
- conv_x: float32 [2, 4, 2048], P('section', None, 'head'), may hold values from -3 to 3
- conv_bc: float32 [2, 4, 2, 128], P('section', None, None, 'head'), may hold values from -3 to 3
- convb_x: float32 [2, 2048], P('section', 'head'), may hold values from -1.8 to 1.8
- convb_bc: float32 [2, 2, 128], P('section', None, 'head'), may hold values from -0.6 to 0.6
- norm_gain: float32 [2, 2048], P('section', 'head'), may hold values from 0.5 to 1.5
- w_out: bfloat16 [2, 2048, 1024], P('section', 'head'), may hold values from -0.125 to 0.125
Outputs:
- ends: float32 [2, 2, 1024, 1024], P('section', None, 'seq')
- g_in_gain: float32 [2, 1024], P('section')
- g_w_z: float32 [2, 1024, 2048], P('section', 'seq', 'head')
- g_w_x: float32 [2, 1024, 2048], P('section', 'seq', 'head')
- g_w_bc: float32 [2, 1024, 2, 128], P('section', 'seq', None, 'head')
- g_w_dt: float32 [2, 1024, 32], P('section', 'seq', 'head')
- g_dt_bias: float32 [2, 32], P('section', 'head')
- g_a_log: float32 [2, 32], P('section', 'head')
- g_skip: float32 [2, 32], P('section', 'head')
- g_conv_x: float32 [2, 4, 2048], P('section', None, 'head')
- g_conv_bc: float32 [2, 4, 2, 128], P('section', None, None, 'head')
- g_convb_x: float32 [2, 2048], P('section', 'head')
- g_convb_bc: float32 [2, 2, 128], P('section', None, 'head')
- g_norm_gain: float32 [2, 2048], P('section', 'head')
- g_w_out: float32 [2, 2048, 1024], P('section', 'head', 'seq')
All inputs are finite; a program needn't handle non-finite values.
Results may differ from a plain program's by a relative error of at most 0.014.
The roundings to bfloat16 on the way count: a program that leaves them out, or rounds other values in their place, can miss the bound.
Values sent between devices are 32-bit elements; how exact they have to be, the bound alone decides.
No kernel may reach another device: no remote copies, remote signals or barrier semaphores. Data moves between devices by JAX's collectives and lax.ppermute only.
A program may use at most 128 MiB of HBM per device.

v0:
```python
import jax
import jax.numpy as jnp
from jax import lax
from jax.sharding import PartitionSpec as P

ED = 2048
HEAD = 64
CONV = 4
STRETCH = 128


EPS = 1e-05
HIGH = lax.Precision.HIGHEST


def from_behind(block, axis, distance):
    devices = range(lax.axis_size(axis))
    route = [(i - distance, i) for i in devices if i - distance in devices]
    return lax.ppermute(block, axis, route)


def entering(part, axis, combine, identity, reverse):
    count = lax.axis_size(axis)
    place = lax.axis_index(axis)
    ahead = count - 1 - place if reverse else place
    gathered = jax.tree.map(lambda a: lax.all_gather(a, axis), part)
    state = jax.tree.map(lambda a, e: jnp.zeros_like(a) + jnp.asarray(e, a.dtype), part, identity)

    def one(lap, state):
        source = count - 1 - lap if reverse else lap
        return combine(
            state, jax.tree.map(lambda a: lax.dynamic_index_in_dim(a, source, 0, False), gathered)
        )

    return lax.fori_loop(0, ahead, one, state)


def matmul_low(left, right):
    return jnp.dot(left, right, preferred_element_type=jnp.float32)


def stretch_step(log_rate, ssm_state, pieces):
    x_stretch, b_stretch, c_stretch, step_stretch = pieces
    stretch_len = x_stretch.shape[0]
    log_cum = jnp.cumsum(step_stretch * log_rate[None, :], axis=0)
    cum_rows = log_cum.T
    lower_mask = jnp.arange(stretch_len)[:, None] >= jnp.arange(stretch_len)[None, :]
    inner_prod = jnp.dot(c_stretch, b_stretch.T, precision=HIGH, preferred_element_type=jnp.float32)
    mix_weights = (
        jnp.where(
            lower_mask[None, :, :],
            jnp.exp(jnp.minimum(cum_rows[:, :, None] - cum_rows[:, None, :], 0.0)),
            0.0,
        )
        * inner_prod[None, :, :]
        * step_stretch.T[:, None, :]
    )
    stretch_out = jnp.einsum("hqk,khp->qhp", mix_weights, x_stretch, precision=HIGH)
    stretch_out = stretch_out + jnp.exp(log_cum)[:, :, None] * jnp.einsum(
        "qn,hpn->qhp", c_stretch, ssm_state, precision=HIGH
    )
    tail_w = jnp.exp(log_cum[-1][None, :] - log_cum) * step_stretch
    new_state = jnp.exp(log_cum[-1])[:, None, None] * ssm_state + jnp.einsum(
        "kh,khp,kn->hpn", tail_w, x_stretch, b_stretch, precision=HIGH
    )
    return (new_state, stretch_out)


def stretch_local(x_ssd, b_ssd, c_ssd, step_size, log_rate):
    tokens_n, heads_loc, head_w = x_ssd.shape
    ssm_state = jnp.zeros((heads_loc, head_w, b_ssd.shape[1]), jnp.float32)
    outputs = []
    for stretch_idx in range(tokens_n // STRETCH):
        row_span = slice(stretch_idx * STRETCH, (stretch_idx + 1) * STRETCH)
        ssm_state, stretch_out = stretch_step(
            log_rate,
            ssm_state,
            (x_ssd[row_span], b_ssd[row_span], c_ssd[row_span], step_size[row_span]),
        )
        outputs.append(stretch_out)
    dec_total = jnp.sum(step_size * log_rate[None, :], axis=0)
    return (jnp.concatenate(outputs, axis=0), dec_total, ssm_state)


def carry_term(c_ssd, step_size, log_rate, entry):
    log_all = jnp.cumsum(step_size * log_rate[None, :], axis=0)
    return jnp.exp(log_all)[:, :, None] * jnp.einsum("tn,hpn->thp", c_ssd, entry, precision=HIGH)


def conv_apply(padded, kernel, shift_b):
    row_count = padded.shape[0] - CONV + 1
    return shift_b[None, :] + sum(
        (kernel[tap][None, :] * padded[tap : tap + row_count] for tap in range(CONV))
    )


def forward_combine(earlier, later):
    return (earlier[0] + later[0], jnp.exp(later[0])[:, None, None] * earlier[1] + later[1])


def backward_combine(earlier, later):
    return (earlier[0] + later[0], later[1] + jnp.exp(later[0])[:, None, None] * earlier[1])


def silu_slope(values):
    sig_val = jax.nn.sigmoid(values)
    return sig_val * (1.0 + values * (1.0 - sig_val))


def forward_block(block_in, weights):
    (
        in_gain,
        w_z,
        w_x,
        w_bc,
        w_dt,
        dt_bias,
        a_log,
        skip,
        conv_x,
        conv_bc,
        convb_x,
        convb_bc,
        norm_gain,
        w_out,
    ) = weights
    tokens_n, model_w = block_in.shape
    inner_w = w_z.shape[1]
    state_loc = w_bc.shape[2]
    heads_loc = w_dt.shape[1]
    in_scale = lax.rsqrt(jnp.mean(block_in * block_in, axis=-1, keepdims=True) + EPS)
    normed = (block_in * in_scale * in_gain[None, :]).astype(jnp.bfloat16)
    gate_in = matmul_low(normed, w_z)
    x_in = matmul_low(normed, w_x)
    bc_in = matmul_low(normed, w_bc.reshape(model_w, 2 * state_loc))
    dt_in = matmul_low(normed, w_dt)
    mixed_in = jnp.concatenate([x_in, bc_in], axis=1)
    edge_rows = from_behind(mixed_in[tokens_n - (CONV - 1) :], "seq", 1)
    padded = jnp.concatenate([edge_rows, mixed_in], axis=0)
    kernel = jnp.concatenate([conv_x, conv_bc.reshape(CONV, 2 * state_loc)], axis=1)
    shift_b = jnp.concatenate([convb_x, convb_bc.reshape(2 * state_loc)])
    conv_out = conv_apply(padded, kernel, shift_b)
    activated = jax.nn.silu(conv_out)
    x_ssd = activated[:, :inner_w].reshape(tokens_n, heads_loc, HEAD)
    bc_loc = activated[:, inner_w:].reshape(tokens_n, 2, state_loc)
    bc_full = lax.all_gather(bc_loc, "head", axis=2, tiled=True)
    b_ssd = bc_full[:, 0]
    c_ssd = bc_full[:, 1]
    step_size = jax.nn.softplus(dt_in + dt_bias[None, :])
    log_rate = -jnp.exp(a_log)
    local_out, dec_total, state_total = stretch_local(x_ssd, b_ssd, c_ssd, step_size, log_rate)
    identity = (jnp.zeros_like(dec_total), jnp.zeros_like(state_total))
    prefix = entering((dec_total, state_total), "seq", forward_combine, identity, False)
    entry = prefix[1]
    ssd_out = (
        local_out + carry_term(c_ssd, step_size, log_rate, entry) + skip[None, :, None] * x_ssd
    )
    ssd_flat = ssd_out.reshape(tokens_n, inner_w)
    gated_out = ssd_flat * jax.nn.silu(gate_in)
    square_sum = lax.psum(jnp.sum(gated_out * gated_out, axis=-1), "head")
    gate_scale = lax.rsqrt(square_sum / ED + EPS)[:, None]
    norm_out = (gated_out * gate_scale * norm_gain[None, :]).astype(jnp.bfloat16)
    branch = lax.psum(matmul_low(norm_out, w_out), "head")
    kept = {
        "block_in": block_in,
        "in_scale": in_scale,
        "normed": normed,
        "gate_in": gate_in,
        "dt_in": dt_in,
        "padded": padded,
        "conv_out": conv_out,
        "x_ssd": x_ssd,
        "b_ssd": b_ssd,
        "c_ssd": c_ssd,
        "step_size": step_size,
        "entry": entry,
        "dec_total": dec_total,
        "ssd_flat": ssd_flat,
        "gated_out": gated_out,
        "gate_scale": gate_scale,
        "norm_out": norm_out,
    }
    return (block_in + branch, kept)


def backward_block(grad_out, kept, weights):
    (
        in_gain,
        w_z,
        w_x,
        w_bc,
        w_dt,
        dt_bias,
        a_log,
        skip,
        conv_x,
        conv_bc,
        convb_x,
        convb_bc,
        norm_gain,
        w_out,
    ) = weights
    block_in = kept["block_in"]
    tokens_n, model_w = block_in.shape
    inner_w = w_z.shape[1]
    state_loc = w_bc.shape[2]
    heads_loc = w_dt.shape[1]
    grad_branch = grad_out.astype(jnp.bfloat16)
    g_w_out = matmul_low(kept["norm_out"].T, grad_branch)
    grad_norm = matmul_low(grad_branch, w_out.T)
    gated_out = kept["gated_out"]
    gate_scale = kept["gate_scale"]
    g_norm_gain = jnp.sum(grad_norm * gated_out * gate_scale, axis=0)
    weighted = grad_norm * norm_gain[None, :]
    cross = lax.psum(jnp.sum(weighted * gated_out, axis=-1), "head")
    grad_gated = gate_scale * weighted - gated_out * gate_scale**3 * cross[:, None] / ED
    gate_in = kept["gate_in"]
    grad_ssd = (grad_gated * jax.nn.silu(gate_in)).reshape(tokens_n, heads_loc, HEAD)
    grad_gate = grad_gated * kept["ssd_flat"] * silu_slope(gate_in)
    x_ssd = kept["x_ssd"]
    b_ssd = kept["b_ssd"]
    c_ssd = kept["c_ssd"]
    step_size = kept["step_size"]
    entry = kept["entry"]
    dec_total = kept["dec_total"]
    log_rate = -jnp.exp(a_log)
    g_skip = jnp.sum(grad_ssd * x_ssd, axis=(0, 2))
    carry_val, carry_back = jax.vjp(carry_term, c_ssd, step_size, log_rate, entry)
    grad_c_one, grad_step_one, grad_rate_one, grad_entry = carry_back(grad_ssd)
    identity = (jnp.zeros_like(dec_total), jnp.zeros_like(grad_entry))
    suffix = entering((dec_total, grad_entry), "seq", backward_combine, identity, True)
    later_grad = suffix[1]
    grad_dec = jnp.exp(dec_total) * jnp.sum(entry * later_grad, axis=(1, 2))
    local_val, local_back = jax.vjp(stretch_local, x_ssd, b_ssd, c_ssd, step_size, log_rate)
    grad_x, grad_b, grad_c_two, grad_step_two, grad_rate_two = local_back(
        (grad_ssd, grad_dec, later_grad)
    )
    grad_x = grad_x + skip[None, :, None] * grad_ssd
    grad_bc_full = jnp.stack([grad_b, grad_c_one + grad_c_two], axis=1)
    grad_bc = lax.psum_scatter(grad_bc_full, "head", scatter_dimension=2, tiled=True)
    grad_step = grad_step_one + grad_step_two
    g_a_log = (grad_rate_one + grad_rate_two) * log_rate
    grad_dt_in = grad_step * jax.nn.sigmoid(kept["dt_in"] + dt_bias[None, :])
    g_dt_bias = jnp.sum(grad_dt_in, axis=0)
    grad_act = jnp.concatenate(
        [grad_x.reshape(tokens_n, inner_w), grad_bc.reshape(tokens_n, 2 * state_loc)], axis=1
    )
    conv_out = kept["conv_out"]
    grad_conv = grad_act * silu_slope(conv_out)
    kernel = jnp.concatenate([conv_x, conv_bc.reshape(CONV, 2 * state_loc)], axis=1)
    shift_b = jnp.concatenate([convb_x, convb_bc.reshape(2 * state_loc)])
    conv_val, conv_back = jax.vjp(conv_apply, kept["padded"], kernel, shift_b)
    grad_pad, g_kernel, g_shift = conv_back(grad_conv)
    from_next = from_behind(grad_pad[: CONV - 1], "seq", -1)
    channels = grad_pad.shape[1]
    grad_mixed = grad_pad[CONV - 1 :] + jnp.concatenate(
        [jnp.zeros((tokens_n - (CONV - 1), channels), jnp.float32), from_next], axis=0
    )
    g_conv_x = g_kernel[:, :inner_w]
    g_conv_bc = g_kernel[:, inner_w:].reshape(CONV, 2, state_loc)
    g_convb_x = g_shift[:inner_w]
    g_convb_bc = g_shift[inner_w:].reshape(2, state_loc)
    gate_low = grad_gate.astype(jnp.bfloat16)
    x_low = grad_mixed[:, :inner_w].astype(jnp.bfloat16)
    bc_low = grad_mixed[:, inner_w:].astype(jnp.bfloat16)
    dt_low = grad_dt_in.astype(jnp.bfloat16)
    normed = kept["normed"]
    g_w_z = matmul_low(normed.T, gate_low)
    g_w_x = matmul_low(normed.T, x_low)
    g_w_bc = matmul_low(normed.T, bc_low).reshape(model_w, 2, state_loc)
    g_w_dt = matmul_low(normed.T, dt_low)
    grad_normed_part = (
        matmul_low(gate_low, w_z.T)
        + matmul_low(x_low, w_x.T)
        + matmul_low(bc_low, w_bc.reshape(model_w, 2 * state_loc).T)
        + matmul_low(dt_low, w_dt.T)
    )
    grad_normed = lax.psum(grad_normed_part, "head")
    in_scale = kept["in_scale"]
    g_in_gain = jnp.sum(grad_normed * block_in * in_scale, axis=0)
    weighted_in = grad_normed * in_gain[None, :]
    grad_in = (
        grad_out
        + in_scale * weighted_in
        - block_in * in_scale**3 * jnp.sum(weighted_in * block_in, axis=-1, keepdims=True) / model_w
    )
    big_grads = (g_w_z, g_w_x, g_w_bc, g_w_dt, g_w_out)
    small_set = (
        g_in_gain,
        g_dt_bias,
        g_a_log,
        g_skip,
        g_conv_x,
        g_conv_bc,
        g_convb_x,
        g_convb_bc,
        g_norm_gain,
    )
    return (grad_in, big_grads, small_set)


def reduce_big(big_grads):
    return (
        lax.psum_scatter(big_grads[0], "seq", scatter_dimension=0, tiled=True),
        lax.psum_scatter(big_grads[1], "seq", scatter_dimension=0, tiled=True),
        lax.psum_scatter(big_grads[2], "seq", scatter_dimension=0, tiled=True),
        lax.psum_scatter(big_grads[3], "seq", scatter_dimension=0, tiled=True),
        lax.psum_scatter(big_grads[4], "seq", scatter_dimension=1, tiled=True),
    )


def on_device(
    inputs,
    cotangent,
    in_gain,
    w_z,
    w_x,
    w_bc,
    w_dt,
    dt_bias,
    a_log,
    skip,
    conv_x,
    conv_bc,
    convb_x,
    convb_bc,
    norm_gain,
    w_out,
):
    section_id = lax.axis_index("section")
    weights = tuple(
        (
            weight[0]
            for weight in (
                in_gain,
                w_z,
                w_x,
                w_bc,
                w_dt,
                dt_bias,
                a_log,
                skip,
                conv_x,
                conv_bc,
                convb_x,
                convb_bc,
                norm_gain,
                w_out,
            )
        )
    )
    micro = inputs.shape[0]
    incoming = jnp.zeros(inputs.shape[1:], jnp.float32)
    kept_all = []
    fwd_outs = []
    for tick in range(micro + 1):
        own_in = inputs[min(tick, micro - 1)].astype(jnp.float32)
        block_in = jnp.where(section_id == 0, own_in, incoming)
        block_out, kept = forward_block(block_in, weights)
        kept_all.append(kept)
        fwd_outs.append(block_out)
        if tick < micro:
            incoming = from_behind(block_out, "section", 1)
    returned = jnp.zeros(inputs.shape[1:], jnp.float32)
    in_grads = []
    big_total = None
    small_total = None
    for tick in range(micro + 1):
        own_cot = cotangent[min(tick, micro - 1)].astype(jnp.float32)
        grad_out = jnp.where(section_id == 1, own_cot, returned)
        upper_kept = kept_all[min(tick + 1, micro)]
        lower_kept = kept_all[max(tick - 1, 0)]
        kept = jax.tree.map(
            lambda first, second: jnp.where(section_id == 1, first, second), upper_kept, lower_kept
        )
        valid = jnp.where(section_id == 1, tick < micro, tick >= 1).astype(jnp.float32)
        grad_in, big_grads, small_set = backward_block(grad_out, kept, weights)
        in_grads.append(grad_in)
        big_grads = tuple((grad * valid for grad in big_grads))
        small_set = tuple((grad * valid for grad in small_set))
        if big_total is None:
            big_total = big_grads
            small_total = small_set
        else:
            big_total = tuple((total + grad for total, grad in zip(big_total, big_grads)))
            small_total = tuple((total + grad for total, grad in zip(small_total, small_set)))
        if tick < micro:
            returned = from_behind(grad_in, "section", -1)
    big_total = reduce_big(big_total)
    small_total = lax.psum(small_total, "seq")
    ends = jnp.stack(
        [
            jnp.where(section_id == 1, fwd_outs[index_mb + 1], in_grads[index_mb + 1])
            for index_mb in range(micro)
        ]
    )[None]
    g_w_z, g_w_x, g_w_bc, g_w_dt, g_w_out = big_total
    (
        g_in_gain,
        g_dt_bias,
        g_a_log,
        g_skip,
        g_conv_x,
        g_conv_bc,
        g_convb_x,
        g_convb_bc,
        g_norm_gain,
    ) = small_total
    return (
        ends,
        g_in_gain[None],
        g_w_z[None],
        g_w_x[None],
        g_w_bc[None],
        g_w_dt[None],
        g_dt_bias[None],
        g_a_log[None],
        g_skip[None],
        g_conv_x[None],
        g_conv_bc[None],
        g_convb_x[None],
        g_convb_bc[None],
        g_norm_gain[None],
        g_w_out[None],
    )


def solution(mesh):
    in_specs = (
        P(None, "seq", None),
        P(None, "seq", None),
        P("section", None),
        P("section", None, "head"),
        P("section", None, "head"),
        P("section", None, None, "head"),
        P("section", None, "head"),
        P("section", "head"),
        P("section", "head"),
        P("section", "head"),
        P("section", None, "head"),
        P("section", None, None, "head"),
        P("section", "head"),
        P("section", None, "head"),
        P("section", "head"),
        P("section", "head", None),
    )
    out_specs = (
        P("section", None, "seq", None),
        P("section", None),
        P("section", "seq", "head"),
        P("section", "seq", "head"),
        P("section", "seq", None, "head"),
        P("section", "seq", "head"),
        P("section", "head"),
        P("section", "head"),
        P("section", "head"),
        P("section", None, "head"),
        P("section", None, None, "head"),
        P("section", "head"),
        P("section", None, "head"),
        P("section", "head"),
        P("section", "head", "seq"),
    )
    return jax.shard_map(
        on_device, mesh=mesh, in_specs=in_specs, out_specs=out_specs, check_vma=False
    )
```

profile of v0, /device:TPU:0, one launch (start us, length us, event | category | flops | bytes accessed | tf_op | source)
XLA Modules:
  0.0 1402.6 jit_solution(15069768118857213251)
XLA Ops:
  12.1 5.5 collective-permute-start
  30.9 9.3 all-reduce.63
  50.1 9.0 all_gather.75
  82.2 10.4 all-gather.19.cloned.1.call-done
  97.3 3.4 multiply_reduce_fusion.19
  100.8 10.0 psum.147
  114.2 55.5 %all-reduce.85.cloned.1.call-done = f32[256,1024]{1,0:T(8,128)} async-done(((f32[256,1024]{1,0:T(8,128)}), f32[256,1024]{1,0:T(8,128)}) %all-reduce.85.cloned.1.call-update) | async-done | bytes 1048592 | tf_op jit(solution)/shard_map/psum | solution.py:163
  205.4 4.2 collective-permute-start.2
  223.2 9.9 all-reduce.64
  238.7 8.9 all_gather.80
  267.0 13.4 all-gather.21.cloned.1.call-done
  288.5 9.9 psum.149
  299.0 3.4 multiply_reduce_fusion.10
  303.9 55.2 %all-reduce.87.cloned.1.call-done = f32[256,1024]{1,0:T(8,128)} async-done(((f32[256,1024]{1,0:T(8,128)}), f32[256,1024]{1,0:T(8,128)}) %all-reduce.87.cloned.1.call-update) | async-done | bytes 1048592 | tf_op jit(solution)/shard_map/psum | solution.py:163
  395.0 4.0 collective-permute-start.6
  440.6 10.4 all-reduce.75
  467.5 9.1 all_gather.88
  504.4 9.9 all-gather.25.cloned.1.call-done
  519.1 3.5 multiply_reduce_fusion.16
  522.6 10.5 all-reduce.72
  560.9 11.0 all-gather.23.cloned.1.call-done
  571.9 5.5 while.80
  598.7 3.6 fusion.507
  643.1 30.1 %all-reduce.93.cloned.1.call-done = f32[256,2,128]{0,1,2:T(2,128)} async-done(((f32[256,2,128]{0,1,2:T(2,128)}), f32[256,2,128]{0,1,2:T(2,128)}) %all-reduce.93.cloned.1.call-update) | async-done | bytes 262160
  674.2 3.6 fusion.95
  679.7 4.0 collective-permute-done.3
  686.2 51.7 %all-reduce.89.cloned.1.call-done = f32[256,1024]{1,0:T(8,128)} async-done(((f32[256,1024]{1,0:T(8,128)}), f32[256,1024]{1,0:T(8,128)}) %all-reduce.89.cloned.1.call-update) | async-done | bytes 1048592 | tf_op jit(solution)/shard_map/psum | solution.py:278
  752.6 8.9 psum.154
  793.3 3.9 all-gather.27.cloned.1.call-done
  797.2 5.7 while.82
  824.2 3.6 fusion.503
  868.5 30.1 %all-reduce.95.cloned.1.call-done = f32[256,2,128]{0,1,2:T(2,128)} async-done(((f32[256,2,128]{0,1,2:T(2,128)}), f32[256,2,128]{0,1,2:T(2,128)}) %all-reduce.95.cloned.1.call-update) | async-done | bytes 262160
  899.6 3.5 fusion.91
  905.1 4.0 collective-permute-done.7
  911.4 51.7 %all-reduce.91.cloned.1.call-done = f32[256,1024]{1,0:T(8,128)} async-done(((f32[256,1024]{1,0:T(8,128)}), f32[256,1024]{1,0:T(8,128)}) %all-reduce.91.cloned.1.call-update) | async-done | bytes 1048592 | tf_op jit(solution)/shard_map/psum | solution.py:278
  965.6 3.4 select_bitcast_fusion.1
  979.9 9.6 psum.157
  989.5 4.2 multiply_reduce_fusion.13
  1034.8 5.5 while.83
  1061.7 3.6 fusion.499
  1103.6 31.7 %all-reduce.97.cloned.1.call-done = f32[256,2,128]{0,1,2:T(2,128)} async-done(((f32[256,2,128]{0,1,2:T(2,128)}), f32[256,2,128]{0,1,2:T(2,128)}) %all-reduce.97.cloned.1.call-update) | async-done | bytes 262160
  1141.1 4.0 collective-permute-done.9
  1174.2 42.3 %all-reduce.99.cloned.1.call-done = (f32[256,1024]{1,0:T(8,128)}, f32[256,1024]{1,0:T(8,128)}) async-done(((f32[256,1024]{1,0:T(8,128)}, f32[256,1024]{1,0:T(8,128)}), (f32[256,1024]{1,0:T(8,128)}, f32[256,1024]{1,0:T(8,128)})) %all-reduce.99.cloned.1.call-update) | async-done | bytes 2097168 | tf_op jit(solution)/shard_map/psum | solution.py:163
  1218.0 19.6 %all-reduce.74 = (f32[1,1024]{1,0:T(1,128)}, f32[1,8]{1,0:T(1,128)}, f32[1,8]{1,0:T(1,128)}, f32[1,8]{1,0:T(1,128)}, f32[1,4,512]{2,1,0:T(4,128)}, /*index=5*/f3...) all-reduce(f32[1,1024]{1,0:T(1,128)S(1)} %bitcast.1104, ...), channel_id=1, replica_groups=mesh['section'=2,'seq'=4,'head'=4] {'seq'}, use_global_device_ids=true, to_apply=%region_129.130 | all-reduce | flops 4440 | bytes 35520 | tf_op jit(solution)/shard_map/psum | solution.py:390
  1241.7 17.0 %reduce-scatter.10.cloned.1.call-done = f32[256,2,32]{0,2,1:T(8,128)} async-done(((f32[1024,2,32]{0,2,1:T(8,128)}), f32[256,2,32]{0,2,1:T(8,128)}) %reduce-scatter.10.cloned.1.call-update) | async-done | bytes 65552 | tf_op jit(solution)/shard_map/reduce_scatter | solution.py:306
  1258.7 44.8 %reduce-scatter.14.cloned.1.call-done = f32[512,256]{1,0:T(8,128)} async-done(((f32[512,1024]{1,0:T(8,128)}), f32[512,256]{1,0:T(8,128)}) %reduce-scatter.14.cloned.1.call-update) | async-done | bytes 524304 | tf_op jit(solution)/shard_map/reduce_scatter | solution.py:308
  1303.5 46.0 %reduce-scatter.6.cloned.1.call-done = f32[256,512]{1,0:T(8,128)} async-done(((f32[1024,512]{1,0:T(8,128)}), f32[256,512]{1,0:T(8,128)}) %reduce-scatter.6.cloned.1.call-update) | async-done | bytes 524304 | tf_op jit(solution)/shard_map/reduce_scatter | solution.py:304
  1349.5 46.1 %reduce-scatter.8.cloned.1.call-done = f32[256,512]{1,0:T(8,128)} async-done(((f32[1024,512]{1,0:T(8,128)}), f32[256,512]{1,0:T(8,128)}) %reduce-scatter.8.cloned.1.call-update) | async-done | bytes 524304 | tf_op jit(solution)/shard_map/reduce_scatter | solution.py:305
  (1267 shorter events, 643.7 us)
Async XLA Ops:
  7.2 105.5 %copy-start = (bf16[1,512,1024]{2,1,0:T(8,128)(2,1)S(1)}, bf16[1,512,1024]{2,1,0:T(8,128)(2,1)}, u32[]{:S(2)}) copy-start(bf16[1,512,1024]{2,1,0:T(8,128)(2,1)} %param.43) | copy-start | bytes 3145732
  7.2 85.3 %all-gather.19.cloned.1.call-start = ((), (), s32[]{:S(2)}) async-start(), calls=%async_computation.14 | async-start | bytes 1310720 | tf_op jit(solution)/shard_map/all_gather | solution.py:26
  12.1 29.7 %collective-permute-start = (f32[3,576]{1,0:T(4,128)}, f32[3,576]{1,0:T(4,128)}, u32[]{:S(2)}, u32[]{:S(2)}) collective-permute-start(f32[3,576]{1,0:T(4,128)} %fusion.519), channel_id=1, source_target_pairs={{0,4},{4,8},{8,12},{1,5},{5,9},{9,13},{2,6},{6,10},{10,14},{3,7},{... | collective-permute-start | bytes 20744 | tf_op jit(solution)/shard_map/ppermute | solution.py:19
  66.8 103.0 %all-reduce.85.cloned.1.call-start = ((), (), s32[]{:S(2)}) async-start(), calls=%async_computation.5 | async-start | bytes 2097152 | tf_op jit(solution)/shard_map/psum | solution.py:163
  114.2 63.6 %copy-start.130 = (f32[1,1024]{1,0:T(1,128)S(1)}, f32[1,1024]{1,0:T(1,128)}, u32[]{:S(2)}) copy-start(f32[1,1024]{1,0:T(1,128)} %param.30) | copy-start | bytes 12292
  114.2 63.6 %copy-start.274 = (f32[256]{0:T(256)S(1)}, f32[256]{0:T(256)}, u32[]{:S(2)}) copy-start(f32[256]{0:T(256)} %copy-done.273) | copy-start | bytes 3076
  114.2 166.2 %all-gather.21.cloned.1.call-start = ((), (), s32[]{:S(2)}) async-start(), calls=%async_computation.15 | async-start | bytes 1310720 | tf_op jit(solution)/shard_map/all_gather | solution.py:26
  172.2 4.3 collective-permute-start.1
  181.1 53.4 %copy-start.21 = (f32[256,512]{1,0:T(8,128)S(1)}, f32[256,512]{1,0:T(8,128)}, u32[]{:S(2)}) copy-start(f32[256,512]{1,0:T(8,128)} %copy-done.20) | copy-start | bytes 1572868
  181.1 53.4 %copy-start.22 = (f32[256,512]{1,0:T(8,128)S(1)}, f32[256,512]{1,0:T(8,128)}, u32[]{:S(2)}) copy-start(f32[256,512]{1,0:T(8,128)} %fusion.65) | copy-start | bytes 1572868
  205.4 29.1 %collective-permute-start.2 = (f32[3,576]{1,0:T(4,128)}, f32[3,576]{1,0:T(4,128)}, u32[]{:S(2)}, u32[]{:S(2)}) collective-permute-start(f32[3,576]{1,0:T(4,128)} %fusion.518), channel_id=1, source_target_pairs={{0,4},{4,8},{8,12},{1,5},{5,9},{9,13},{2,6},{6,10},{10,14},{3,7},{... | collective-permute-start | bytes 20744 | tf_op jit(solution)/shard_map/ppermute | solution.py:19
  254.6 104.6 %all-reduce.87.cloned.1.call-start = ((), (), s32[]{:S(2)}) async-start(), calls=%async_computation.6 | async-start | bytes 2097152 | tf_op jit(solution)/shard_map/psum | solution.py:163
  257.5 22.9 %copy-start.85 = (f32[256,1,128]{2,0,1:T(8,128)}, f32[256,1,128]{2,0,1:T(8,128)S(1)}, u32[]{:S(2)}) copy-start(f32[256,1,128]{2,0,1:T(8,128)S(1)} %copy.715) | copy-start | bytes 393220
  285.7 13.3 copy-start.195
  303.9 210.4 %all-gather.25.cloned.1.call-start = ((), (), s32[]{:S(2)}) async-start(), calls=%async_computation.17 | async-start | bytes 1310720 | tf_op jit(solution)/shard_map/all_gather | solution.py:26
  360.6 9.9 collective-permute-start.5
  379.1 83.3 %copy-start.115 = (f32[256,64]{1,0:T(8,128)S(1)}, f32[256,64]{1,0:T(8,128)}, u32[]{:S(2)}) copy-start(f32[256,64]{1,0:T(8,128)} %fusion.647) | copy-start | bytes 196612
  395.0 67.5 %collective-permute-start.6 = (f32[3,576]{1,0:T(4,128)}, f32[3,576]{1,0:T(4,128)}, u32[]{:S(2)}, u32[]{:S(2)}) collective-permute-start(f32[3,576]{1,0:T(4,128)} %fusion.517), channel_id=1, source_target_pairs={{0,4},{4,8},{8,12},{1,5},{5,9},{9,13},{2,6},{6,10},{10,14},{3,7},{... | collective-permute-start | bytes 20744 | tf_op jit(solution)/shard_map/ppermute | solution.py:19
  488.5 83.3 %all-gather.23.cloned.1.call-start = ((), (), s32[]{:S(2)}) async-start(), calls=%async_computation.16 | async-start | bytes 1310720 | tf_op jit(solution)/shard_map/all_gather | solution.py:26
  540.8 132.4 %all-reduce.93.cloned.1.call-start = ((), (), s32[]{:S(2)}) async-start(), calls=%async_computation.20 | async-start | bytes 524288
  632.0 105.9 %all-reduce.89.cloned.1.call-start = ((), (), s32[]{:S(2)}) async-start(), calls=%async_computation.7 | async-start | bytes 2097152 | tf_op jit(solution)/shard_map/psum | solution.py:278
  678.1 5.7 collective-permute-start.3
  684.7 53.2 %copy-start.132 = (f32[1,1024]{1,0:T(1,128)S(1)}, f32[1,1024]{1,0:T(1,128)}, u32[]{:S(2)}) copy-start(f32[1,1024]{1,0:T(1,128)} %param.30) | copy-start | bytes 12292
  684.7 53.2 %copy-start.278 = (f32[256]{0:T(256)S(1)}, f32[256]{0:T(256)}, u32[]{:S(2)}) copy-start(f32[256]{0:T(256)} %get-tuple-element.790) | copy-start | bytes 3076
  686.1 54.3 %copy-start.306 = (f32[256]{0:T(256)S(1)}, f32[256]{0:T(256)}, u32[]{:S(2)}) copy-start(f32[256]{0:T(256)} %get-tuple-element.789) | copy-start | bytes 3076
  686.1 111.1 %all-gather.27.cloned.1.call-start = ((), (), s32[]{:S(2)}) async-start(), calls=%async_computation.18 | async-start | bytes 1310720 | tf_op jit(solution)/shard_map/all_gather | solution.py:26
  743.1 5.8 collective-permute-start.4
  769.1 129.6 %all-reduce.95.cloned.1.call-start = ((), (), s32[]{:S(2)}) async-start(), calls=%async_computation.21 | async-start | bytes 524288
  857.4 105.8 %all-reduce.91.cloned.1.call-start = ((), (), s32[]{:S(2)}) async-start(), calls=%async_computation.8 | async-start | bytes 2097152 | tf_op jit(solution)/shard_map/psum | solution.py:278
  903.4 5.7 collective-permute-start.7
  910.0 53.2 %copy-start.133 = (f32[1,1024]{1,0:T(1,128)S(1)}, f32[1,1024]{1,0:T(1,128)}, u32[]{:S(2)}) copy-start(f32[1,1024]{1,0:T(1,128)} %param.30) | copy-start | bytes 12292
  910.0 53.2 %copy-start.277 = (f32[256]{0:T(256)S(1)}, f32[256]{0:T(256)}, u32[]{:S(2)}) copy-start(f32[256]{0:T(256)} %get-tuple-element.788) | copy-start | bytes 3076
  911.4 54.2 %copy-start.305 = (f32[256]{0:T(256)S(1)}, f32[256]{0:T(256)}, u32[]{:S(2)}) copy-start(f32[256]{0:T(256)} %get-tuple-element.787) | copy-start | bytes 3076
  911.4 123.4 %all-gather.29.cloned.1.call-start = ((), (), s32[]{:S(2)}) async-start(), calls=%async_computation.19 | async-start | bytes 1310720 | tf_op jit(solution)/shard_map/all_gather | solution.py:26
  969.0 5.7 collective-permute-start.8
  979.9 53.4 %copy-start.60 = (bf16[256,512]{1,0:T(8,128)(2,1)}, bf16[256,512]{1,0:T(8,128)(2,1)S(1)}, u32[]{:S(2)}) copy-start(bf16[256,512]{1,0:T(8,128)(2,1)S(1)} %get-tuple-element.680) | copy-start | bytes 786436
  999.8 135.5 %all-reduce.97.cloned.1.call-start = ((), (), s32[]{:S(2)}) async-start(), calls=%async_computation.22 | async-start | bytes 524288
  1095.0 121.4 %all-reduce.99.cloned.1.call-start = ((), (), s32[]{:S(2)}) async-start(), calls=%async_computation.23 | async-start | bytes 4194304 | tf_op jit(solution)/shard_map/psum | solution.py:163
  1139.4 5.7 collective-permute-start.9
  1147.4 94.3 %reduce-scatter.12.cloned.1.call-start = ((), (), s32[]{:S(2)}) async-start(), calls=%async_computation.12 | async-start | bytes 40960 | tf_op jit(solution)/shard_map/reduce_scatter | solution.py:307
  1155.0 103.7 %reduce-scatter.10.cloned.1.call-start = ((), (), s32[]{:S(2)}) async-start(), calls=%async_computation.11 | async-start | bytes 327680 | tf_op jit(solution)/shard_map/reduce_scatter | solution.py:306
  1157.1 146.4 %reduce-scatter.14.cloned.1.call-start = ((), (), s32[]{:S(2)}) async-start(), calls=%async_computation.13 | async-start | bytes 2621440 | tf_op jit(solution)/shard_map/reduce_scatter | solution.py:308
  1161.2 188.4 %reduce-scatter.6.cloned.1.call-start = ((), (), s32[]{:S(2)}) async-start(), calls=%async_computation.9 | async-start | bytes 2621440 | tf_op jit(solution)/shard_map/reduce_scatter | solution.py:304
  1166.7 229.0 %reduce-scatter.8.cloned.1.call-start = ((), (), s32[]{:S(2)}) async-start(), calls=%async_computation.10 | async-start | bytes 2621440 | tf_op jit(solution)/shard_map/reduce_scatter | solution.py:305
  1172.5 44.0 %copy-start.276 = (f32[256]{0:T(256)S(1)}, f32[256]{0:T(256)}, u32[]{:S(2)}) copy-start(f32[256]{0:T(256)} %get-tuple-element.593) | copy-start | bytes 3076
  1172.5 45.5 %copy-start.240 = (f32[1024]{0:T(1024)S(1)}, f32[1024]{0:T(1024)}, u32[]{:S(2)}) copy-start(f32[1024]{0:T(1024)} %get-tuple-element.405) | copy-start | bytes 12292
  1172.5 45.5 %copy-start.241 = (f32[1024]{0:T(1024)S(1)}, f32[1024]{0:T(1024)}, u32[]{:S(2)}) copy-start(f32[1024]{0:T(1024)} %get-tuple-element.407) | copy-start | bytes 12292
  1172.5 65.1 %copy-start.304 = (f32[256]{0:T(256)S(1)}, f32[256]{0:T(256)}, u32[]{:S(2)}) copy-start(f32[256]{0:T(256)} %get-tuple-element.592) | copy-start | bytes 3076
  (312 other events, 1676.1 us)
Sparse Core Ops, SparseCore 0:
  66.9 25.6 all-gather.18
  114.3 55.4 all-reduce.84
  254.7 25.6 all-gather.20
  304.0 55.1 all-reduce.86
  488.6 25.6 all-gather.24
  540.9 30.8 all-gather.22
  632.1 41.0 all-reduce.92
  686.2 51.6 all-reduce.88
  769.2 27.9 all-gather.26
  857.5 41.0 all-reduce.94
  911.5 51.6 all-reduce.90
  999.9 27.9 all-gather.28
  1095.2 40.1 all-reduce.96
  1147.5 68.9 all-reduce.98
  1219.1 18.9 reduce-scatter.11
  1240.9 17.7 reduce-scatter.9
  1261.4 42.0 reduce-scatter.13
  1306.3 43.1 reduce-scatter.5
  1352.4 43.1 reduce-scatter.7
where the time goes:
time: 1420 us; the launch traced here: 1400 us
  waiting for transfers between devices  565 us (40%)
  local copies, waits for them, and re-layouts  236 us (17%)
  matrix products  225 us (16%)
  other arithmetic  204 us (14%)
  blocking collectives  125 us (9%)
  starting transfers between devices  26.9 us (2%)
  between operations  19.9 us (1%)
    psum x3, waiting for transfers between devices, forward_block(): branch = lax.psum(matmul_low(norm_out, w_out), 'head')  153 us
    psum x2, waiting for transfers between devices, backward_block(): grad_normed = lax.psum(grad_normed_part, 'head')  103 us
    unnamed x22, waiting for transfers between devices  92.3 us
    dot_general x45, matrix products, matmul_low(): return jnp.dot(left, right, preferred_element_type=jnp.float32)  64.6 us
    all_gather x6, waiting for transfers between devices, entering(): gathered = jax.tree.map(lambda a: lax.all_gather(a, axis), part)  48.6 us
    dot_general x18, matrix products, stretch_step(): jnp.einsum('hqk,khp->qhp', mix_weights, x_stretch, precision=HIGH)  47.4 us
    reduce_scatter x1, waiting for transfers between devices, reduce_big(): lax.psum_scatter(big_grads[1], 'seq', scatter_dimension=0, tiled=True)  46.1 us
    reduce_scatter x1, waiting for transfers between devices, reduce_big(): lax.psum_scatter(big_grads[0], 'seq', scatter_dimension=0, tiled=True)  46 us
  transfers between devices with their start and end apart: 29, of which 21 were waited for; matrix products, arithmetic and copies ran while one was open for 20% of the time, Pallas kernels for 0%

commit v1 on v0

v1 whole, which is shorter than its diff:
```python
import functools

import jax
import jax.numpy as jnp
from jax import lax
from jax.experimental import pallas as pl
from jax.experimental.pallas import tpu as pltpu
from jax.sharding import PartitionSpec as P

ED = 2048
HEAD = 64
CONV = 4
EPS = 1e-05
EDGE = 8
LANES = 128
F32 = jnp.float32
BF16 = jnp.bfloat16
NN = (((1,), (0,)), ((), ()))
NT = (((1,), (1,)), ((), ()))
TN = (((0,), (0,)), ((), ()))


def dot_low(left, right, dims=NN):
    return lax.dot_general(left.astype(BF16), right.astype(BF16), dims, preferred_element_type=F32)


def halves(value):
    high = value.astype(BF16)
    return high, (value - high.astype(F32)).astype(BF16)


def dot_split(left, right, dims=NN):
    left_hi, left_lo = halves(left)
    right_hi, right_lo = halves(right)
    mul = functools.partial(lax.dot_general, dimension_numbers=dims, preferred_element_type=F32)
    return mul(left_hi, right_hi) + (mul(left_hi, right_lo) + mul(left_lo, right_hi))


def dot_exact(left, right, dims=NN):
    return lax.dot_general(
        left, right, dims, precision=lax.Precision.HIGHEST, preferred_element_type=F32
    )


dot_mix = dot_split
dot_sum = dot_exact


def kernel_call(body, outs, args, time_us, scratch=(), scalars=True):
    specs = [pl.BlockSpec(memory_space=pltpu.VMEM)] * len(args)
    if scalars:
        specs[0] = pl.BlockSpec(memory_space=pltpu.SMEM)
    return pl.pallas_call(
        body,
        out_shape=[jax.ShapeDtypeStruct(shape, dtype) for shape, dtype in outs],
        in_specs=specs,
        out_specs=[pl.BlockSpec(memory_space=pltpu.VMEM)] * len(outs),
        scratch_shapes=list(scratch),
        compiler_params=pltpu.CompilerParams(vmem_limit_bytes=40 * 1024 * 1024),
        cost_estimate=pl.CostEstimate(
            flops=0, bytes_accessed=int(time_us * 3_000_000), transcendentals=0
        ),
    )(*args)


def sigmoid(values):
    return 1.0 / (1.0 + jnp.exp(-values))


def softplus(values):
    return jnp.maximum(values, 0.0) + jnp.log1p(jnp.exp(-jnp.abs(values)))


def one_hot(channels):
    head_of = lax.broadcasted_iota(jnp.int32, (channels, LANES), 0) // HEAD
    return (head_of == lax.broadcasted_iota(jnp.int32, (channels, LANES), 1)).astype(F32)


def spread(per_head, channels):
    rows = per_head.shape[0]
    return jnp.concatenate(
        [
            jnp.broadcast_to(per_head[:, head : head + 1], (rows, HEAD))
            for head in range(channels // HEAD)
        ],
        axis=1,
    )


def ordered(tokens):
    row = lax.broadcasted_iota(jnp.int32, (tokens, tokens), 0)
    col = lax.broadcasted_iota(jnp.int32, (tokens, tokens), 1)
    return row >= col


def place(scalars_ref, half, part, parts, rows):
    section = scalars_ref[0]
    head = scalars_ref[1]
    side = section if half == 0 else 1 - section
    start = (side * parts + jnp.bitwise_xor(head, part)) * rows
    return pl.multiple_of(start, rows)


def gather_rows(scalars_ref, target_ref, own_ref, other_ref, parts):
    rows = own_ref.shape[0] // parts
    for half, source in enumerate((own_ref, other_ref)):
        for part in range(parts):
            start = place(scalars_ref, half, part, parts, rows)
            target_ref[pl.ds(start, rows), :] = source[part * rows : (part + 1) * rows, :]


def deal_rows(scalars_ref, source_ref, keep_ref, send_ref, parts):
    rows = keep_ref.shape[0] // parts
    for half, target in enumerate((keep_ref, send_ref)):
        for part in range(parts):
            start = place(scalars_ref, half, part, parts, rows)
            target[part * rows : (part + 1) * rows, :] = source_ref[pl.ds(start, rows), :]


def pick_weights(
    where_ref, z_ref, x_ref, out_ref, got_zx_ref, got_out_ref, own_pack_ref, other_pack_ref,
    zx0_ref, zx1_ref, bc0_ref, bc1_ref, dt0_ref, dt1_ref, out0_ref, out1_ref, *, heads_n
):
    section = where_ref[0]
    model_w = z_ref.shape[0]
    inner = zx0_ref.shape[1] // 2
    channels = bc0_ref.shape[1]
    here = pl.ds(pl.multiple_of(section * inner, inner), inner)
    lane = lax.broadcasted_iota(jnp.int32, (model_w, LANES), 1)

    def narrow(pack_ref):
        both = pack_ref[:model_w, channels:]
        side = jnp.where(section == 0, both, pltpu.roll(both, LANES - heads_n, 1))
        return jnp.where(lane < heads_n, side, 0.0).astype(BF16)

    own = (z_ref[:, here], x_ref[:, here])
    got = (got_zx_ref[:, :inner].astype(BF16), got_zx_ref[:, inner:].astype(BF16))
    own_out = out_ref[here, :]
    got_out = got_out_ref[...].astype(BF16)
    own_bc = own_pack_ref[:model_w, :channels].astype(BF16)
    other_bc = other_pack_ref[:model_w, :channels].astype(BF16)
    own_dt = narrow(own_pack_ref)
    other_dt = narrow(other_pack_ref)

    def write(first, second):
        for source, refs in (
            (first, (zx0_ref, bc0_ref, dt0_ref, out0_ref)),
            (second, (zx1_ref, bc1_ref, dt1_ref, out1_ref)),
        ):
            zx_from, bc_from, dt_from, out_from = source
            refs[0][:, :inner] = zx_from[0]
            refs[0][:, inner:] = zx_from[1]
            refs[1][...] = bc_from
            refs[2][...] = dt_from
            refs[3][...] = out_from

    own_set = (own, own_bc, own_dt, own_out)
    got_set = (got, other_bc, other_dt, got_out)

    @pl.when(section == 0)
    def _():
        write(own_set, got_set)

    @pl.when(section != 0)
    def _():
        write(got_set, own_set)


def project(block_in, halo, in_gain, w_zx, w_bc, w_dt, taps, heads, outs):
    normed_ref, gate_ref, pad_ref, conv_ref, dt_ref, cum_ref, local_ref, state_ref = outs
    tokens = block_in.shape[0]
    inner = w_zx.shape[1] // 2
    rows = jnp.concatenate([halo, block_in], axis=0)
    scale = lax.rsqrt(jnp.mean(rows * rows, axis=-1, keepdims=True) + EPS)
    normed = (rows * scale * in_gain).astype(BF16)
    low = normed[EDGE:]
    normed_ref[...] = low
    gate_ref[...] = dot_low(low, w_zx[:, :inner])
    pad_ref[:, :inner] = dot_low(normed, w_zx[:, inner:])
    pad_ref[:, inner:] = dot_low(normed, w_bc)
    dt_val = dot_low(low, w_dt) + heads[0:1, :]
    dt_ref[...] = dt_val
    conv = taps[CONV : CONV + 1, :]
    for tap in range(CONV):
        first = EDGE - CONV + 1 + tap
        conv = conv + taps[tap : tap + 1, :] * pad_ref[first : first + tokens, :]
    conv_ref[...] = conv
    act = conv * sigmoid(conv)
    state_w = (act.shape[1] - inner) // 2
    x_ssd = act[:, :inner]
    b_ssd = act[:, inner : inner + state_w]
    c_ssd = act[:, inner + state_w :]
    log_rate = -jnp.exp(heads[1:2, :])
    step = softplus(dt_val)
    lower = ordered(tokens)
    cum = dot_sum(lower.astype(F32), step * log_rate)
    cum_ref[...] = cum
    cum_rows = cum.T
    scaled = x_ssd * spread(step, inner)
    cross = jnp.where(lower, dot_mix(c_ssd, b_ssd, NT), 0.0)
    outputs = []
    for head in range(inner // HEAD):
        gap = cum[:, head : head + 1] - cum_rows[head : head + 1, :]
        mix = cross * jnp.exp(jnp.minimum(gap, 0.0))
        outputs.append(dot_mix(mix, scaled[:, head * HEAD : (head + 1) * HEAD]))
    local_ref[...] = jnp.concatenate(outputs, axis=1) + spread(heads[2:3, :], inner) * x_ssd
    cum_chan = spread(cum, inner)
    last = cum_chan[tokens - 1 : tokens, :]
    state_ref[:state_w, :] = dot_mix(b_ssd, scaled * jnp.exp(last - cum_chan), TN)
    state_ref[state_w:, :] = jnp.broadcast_to(last, (EDGE, inner))


def first_forward(in_ref, halo_ref, gain_ref, zx_ref, bc_ref, dt_ref, taps_ref, heads_ref, *outs):
    project(
        in_ref[...].astype(F32), halo_ref[...], gain_ref[...], zx_ref[...], bc_ref[...],
        dt_ref[...], taps_ref[...], heads_ref[...], outs,
    )


def later_forward(
    parts, where_ref, own_ref, other_ref, halo_ref, gain_ref, zx_ref, bc_ref, dt_ref, taps_ref,
    heads_ref, in_ref, *outs
):
    gather_rows(where_ref, in_ref, own_ref, other_ref, parts)
    project(
        in_ref[...], halo_ref[...], gain_ref[...], zx_ref[...], bc_ref[...], dt_ref[...],
        taps_ref[...], heads_ref[...], outs,
    )


def mixed_output(local_ref, entry_ref, conv_ref, cum_ref, gate_ref):
    inner = local_ref.shape[1]
    state_w = entry_ref.shape[0] - EDGE
    conv_c = conv_ref[:, inner + state_w :]
    c_ssd = conv_c * sigmoid(conv_c)
    grown = jnp.exp(spread(cum_ref[...], inner))
    ssd = local_ref[...] + grown * dot_mix(c_ssd, entry_ref[:state_w, :])
    gate = gate_ref[...]
    return ssd, ssd * (gate * sigmoid(gate))


def sums_of(squares, inner_prod):
    lane = lax.broadcasted_iota(jnp.int32, (squares.shape[0], LANES), 1)
    both = jnp.where(lane == 0, squares, jnp.where(lane == 1, inner_prod, 0.0))
    return both.T[:EDGE, :]


def rate_of(sums):
    fill = jnp.zeros((LANES - sums.shape[0], sums.shape[1]), F32)
    columns = jnp.concatenate([sums, fill], axis=0).T
    return lax.rsqrt(columns[:, :1] / ED + EPS), columns[:, 1:2]


def first_output(local_ref, entry_ref, conv_ref, cum_ref, gate_ref, ssd_ref, sums_ref):
    ssd, gated = mixed_output(local_ref, entry_ref, conv_ref, cum_ref, gate_ref)
    ssd_ref[...] = ssd
    sums_ref[...] = sums_of(jnp.sum(gated * gated, axis=-1, keepdims=True), 0.0)


def first_branch(
    parts, where_ref, sums_ref, ssd_ref, gate_ref, gain_ref, w_out_ref, norm_ref, keep_ref,
    send_ref, whole_ref
):
    rate, _ = rate_of(sums_ref[...])
    gate = gate_ref[...]
    norm_out = (ssd_ref[...] * (gate * sigmoid(gate)) * rate * gain_ref[...]).astype(BF16)
    norm_ref[...] = norm_out
    whole_ref[...] = dot_low(norm_out, w_out_ref[...])
    deal_rows(where_ref, whole_ref, keep_ref, send_ref, parts)


def second_output(
    local_ref, entry_ref, conv_ref, cum_ref, gate_ref, gain_ref, w_out_ref, cot_ref,
    ssd_ref, grad_norm_ref, sums_ref
):
    ssd, gated = mixed_output(local_ref, entry_ref, conv_ref, cum_ref, gate_ref)
    ssd_ref[...] = ssd
    grad_norm = dot_low(cot_ref[...], w_out_ref[...], NT)
    grad_norm_ref[...] = grad_norm
    squares = jnp.sum(gated * gated, axis=-1, keepdims=True)
    inner_prod = jnp.sum(grad_norm * gain_ref[...] * gated, axis=-1, keepdims=True)
    sums_ref[...] = sums_of(squares, inner_prod)


def add_plain(base_ref, own_ref, *refs):
    *got, out_ref = refs
    total = own_ref[...]
    for ref in got:
        total = total + ref[...]
    out_ref[...] = base_ref[...] + total


def gate_back(grad_norm, rate, cross, ssd, gate, gain, conv, cum, state, outs):
    dy_ref, dz_ref, norm_ref, grow_ref, entry_ref = outs
    inner = ssd.shape[1]
    state_w = (conv.shape[1] - inner) // 2
    sig = sigmoid(gate)
    silu = gate * sig
    gated = ssd * silu
    unit = gated * rate
    norm_ref[...] = (unit * gain).astype(BF16)
    grow_ref[...] = jnp.broadcast_to(
        jnp.sum(grad_norm * unit, axis=0, keepdims=True), (EDGE, inner)
    )
    grad_gated = rate * (grad_norm * gain) - unit * (rate * rate * cross / ED)
    dy = grad_gated * silu
    dy_ref[...] = dy
    dz_ref[...] = (grad_gated * ssd * (sig * (1.0 + gate * (1.0 - sig)))).astype(BF16)
    conv_c = conv[:, inner + state_w :]
    c_ssd = conv_c * sigmoid(conv_c)
    grown = jnp.exp(spread(cum, inner))
    entry_ref[:state_w, :] = dot_mix(c_ssd, grown * dy, TN)
    entry_ref[state_w:, :] = state[state_w:, :]


def second_gate(
    sums_ref, grad_norm_ref, ssd_ref, gate_ref, gain_ref, conv_ref, cum_ref, state_ref, *outs
):
    rate, cross = rate_of(sums_ref[...])
    gate_back(
        grad_norm_ref[...], rate, cross, ssd_ref[...], gate_ref[...], gain_ref[...],
        conv_ref[...], cum_ref[...], state_ref[...], outs,
    )


def first_gate(
    parts, where_ref, own_ref, other_ref, after_ref, before_ref, sums_ref, w_out_ref, ssd_ref,
    gate_ref, gain_ref, conv_ref, cum_ref, state_ref, low_ref, *outs
):
    *outs, whole_ref = outs
    gather_rows(where_ref, whole_ref, own_ref, other_ref, parts)
    grad_low = whole_ref[...].astype(BF16)
    low_ref[...] = grad_low
    grad_norm = dot_low(grad_low, w_out_ref[...], NT)
    rate, _ = rate_of(sums_ref[...])
    branch = after_ref[...] - before_ref[...].astype(F32)
    cross = jnp.sum(grad_low.astype(F32) * branch, axis=-1, keepdims=True) / rate
    gate_back(
        grad_norm, rate, cross, ssd_ref[...], gate_ref[...], gain_ref[...], conv_ref[...],
        cum_ref[...], state_ref[...], outs,
    )


def out_project(parts, where_ref, norm_ref, w_out_ref, keep_ref, send_ref, whole_ref):
    whole_ref[...] = dot_low(norm_ref[...], w_out_ref[...])
    deal_rows(where_ref, whole_ref, keep_ref, send_ref, parts)


def scan_back(
    dy_ref, ssd_ref, conv_ref, pad_ref, dt_ref, cum_ref, entry_ref, state_ref, later_ref,
    taps_ref, heads_ref, mixed_ref, ddt_ref, small_ref, heads_out_ref, line_ref
):
    tokens, inner = dy_ref.shape
    state_w = entry_ref.shape[0] - EDGE
    dy = dy_ref[...]
    conv = conv_ref[...]
    sig = sigmoid(conv)
    act = conv * sig
    x_ssd = act[:, :inner]
    b_ssd = act[:, inner : inner + state_w]
    c_ssd = act[:, inner + state_w :]
    heads = heads_ref[...]
    log_rate = -jnp.exp(heads[1:2, :])
    skip = spread(heads[2:3, :], inner)
    dt_val = dt_ref[...]
    step = softplus(dt_val)
    cum = cum_ref[...]
    cum_rows = cum.T
    cum_chan = spread(cum, inner)
    step_chan = spread(step, inner)
    last = cum_chan[tokens - 1 : tokens, :]
    tail = jnp.exp(last - cum_chan)
    scaled = x_ssd * step_chan
    entry = entry_ref[:state_w, :]
    later = later_ref[:state_w, :]
    lower = ordered(tokens)
    cross = jnp.where(lower, dot_mix(c_ssd, b_ssd, NT), 0.0)
    grad_cross = jnp.zeros((tokens, tokens), F32)
    grad_scaled = []
    for head in range(inner // HEAD):
        span = slice(head * HEAD, (head + 1) * HEAD)
        gap = cum[:, head : head + 1] - cum_rows[head : head + 1, :]
        decay = jnp.exp(jnp.minimum(gap, 0.0))
        grad_scaled.append(dot_mix(cross * decay, dy[:, span], TN))
        grad_cross = grad_cross + decay * dot_mix(dy[:, span], scaled[:, span], NT)
    grad_cross = jnp.where(lower, grad_cross, 0.0)
    grad_scaled = jnp.concatenate(grad_scaled, axis=1) + tail * dot_mix(b_ssd, later)
    grad_c = dot_mix(grad_cross, b_ssd) + dot_mix(jnp.exp(cum_chan) * dy, entry, NT)
    grad_b = dot_mix(grad_cross, c_ssd, TN) + dot_mix(tail * scaled, later, NT)
    grad_x = step_chan * grad_scaled + skip * dy
    hot = one_hot(inner)
    dx_prod = x_ssd * grad_scaled
    dy_x = dy * x_ssd
    grad_cum = dot_sum(dy * ssd_ref[...] - skip * dy_x - step_chan * dx_prod, hot)
    final = jnp.exp(last) * entry + state_ref[:state_w, :]
    at_end = jnp.broadcast_to(jnp.sum(later * final, axis=0, keepdims=True), (EDGE, inner))
    behind = dot_sum(lower.astype(F32), grad_cum, TN) + dot_sum(at_end, hot)[:1, :]
    grad_step = behind * log_rate + dot_sum(dx_prod, hot)
    grad_dt = grad_step * sigmoid(dt_val)
    ddt_ref[...] = grad_dt.astype(BF16)
    skip_sum = jnp.broadcast_to(jnp.sum(dy_x, axis=0, keepdims=True), (EDGE, inner))
    row = lax.broadcasted_iota(jnp.int32, (EDGE, LANES), 0)
    heads_out_ref[...] = jnp.where(
        row == 0,
        jnp.sum(grad_dt, axis=0, keepdims=True),
        jnp.where(
            row == 1,
            jnp.sum(step * behind, axis=0, keepdims=True) * log_rate,
            jnp.where(row == 2, dot_sum(skip_sum, hot), 0.0),
        ),
    )
    grad_conv = jnp.concatenate([grad_x, grad_b, grad_c], axis=1) * (
        sig * (1.0 + conv * (1.0 - sig))
    )
    channels = conv.shape[1]
    line_ref[: 2 * EDGE, :] = jnp.zeros((2 * EDGE, channels), F32)
    line_ref[2 * EDGE : 2 * EDGE + tokens, :] = grad_conv
    line_ref[2 * EDGE + tokens :, :] = jnp.zeros((EDGE, channels), F32)
    mixed = jnp.zeros((tokens + EDGE, channels), F32)
    for tap in range(CONV):
        first = EDGE + CONV - 1 - tap
        mixed = mixed + taps_ref[tap : tap + 1, :] * line_ref[first : first + tokens + EDGE, :]
        first = EDGE - CONV + 1 + tap
        small_ref[tap : tap + 1, :] = jnp.sum(
            grad_conv * pad_ref[first : first + tokens, :], axis=0, keepdims=True
        )
    small_ref[CONV : CONV + 1, :] = jnp.sum(grad_conv, axis=0, keepdims=True)
    small_ref[CONV + 1 :, :] = jnp.zeros((EDGE - CONV - 1, channels), F32)
    mixed_ref[...] = mixed


def normed_back(
    parts, where_ref, mixed_ref, next_ref, dz_ref, ddt_ref, zx_ref, bc_ref, dt_ref, in_ref,
    x_low_ref, bc_ref_out, gain_ref, keep_ref, send_ref, whole_ref
):
    tokens = mixed_ref.shape[0] - EDGE
    inner = dz_ref.shape[1]
    fill = jnp.zeros((tokens - EDGE, mixed_ref.shape[1]), F32)
    mixed = mixed_ref[EDGE:, :] + jnp.concatenate([fill, next_ref[...]], axis=0)
    x_low = mixed[:, :inner].astype(BF16)
    x_low_ref[...] = x_low
    grad_bc = mixed[:, inner:]
    bc_ref_out[...] = grad_bc
    high, rest = halves(grad_bc)
    total = (
        dot_low(dz_ref[...], zx_ref[:, :inner], NT)
        + dot_low(x_low, zx_ref[:, inner:], NT)
        + dot_low(high, bc_ref[...], NT)
        + dot_low(rest, bc_ref[...], NT)
        + dot_low(ddt_ref[...], dt_ref[...], NT)
    )
    whole_ref[...] = total
    block_in = in_ref[...].astype(F32)
    scale = lax.rsqrt(jnp.mean(block_in * block_in, axis=-1, keepdims=True) + EPS)
    gain_ref[...] = jnp.broadcast_to(
        jnp.sum(total * block_in * scale, axis=0, keepdims=True), (EDGE, total.shape[1])
    )
    deal_rows(where_ref, whole_ref, keep_ref, send_ref, parts)


def input_back(grad_ref, in_ref, gain_ref, own_ref, *refs):
    *got, out_ref = refs
    total = own_ref[...]
    for ref in got:
        total = total + ref[...]
    block_in = in_ref[...]
    scale = lax.rsqrt(jnp.mean(block_in * block_in, axis=-1, keepdims=True) + EPS)
    weighted = total * gain_ref[...]
    inner_prod = jnp.mean(weighted * block_in, axis=-1, keepdims=True)
    out_ref[...] = (
        grad_ref[...] + scale * weighted - block_in * (scale * scale * scale * inner_prod)
    )


def lay_out(parts, where_ref, *refs):
    *pieces, out_ref = refs
    section = where_ref[0]
    micro = out_ref.shape[0]
    rows = pieces[0].shape[0] // parts
    for index in range(micro):
        lower = pieces[2 * index : 2 * index + 2]
        upper = pieces[2 * (micro + index) : 2 * (micro + index) + 2]
        for half in range(2):
            for part in range(parts):
                span = slice(part * rows, (part + 1) * rows)
                start = place(where_ref, half, part, parts, rows)
                out_ref[index, pl.ds(start, rows), :] = jnp.where(
                    section == 0, lower[half][span, :], upper[half][span, :]
                )


def swap(block):
    return lax.ppermute(block, "section", [(0, 1), (1, 0)])


def across(block, mask):
    count = lax.axis_size("head")
    return lax.ppermute(block, "head", [(i, i ^ mask) for i in range(count)])


def along(block, distance):
    devices = range(lax.axis_size("seq"))
    return lax.ppermute(
        block, "seq", [(i, i + distance) for i in devices if i + distance in devices]
    )


def carried(own, direction):
    depth = own.shape[0] - EDGE

    def combine(near, far):
        decay = near[depth : depth + 1]
        return jnp.concatenate(
            [near[:depth] + jnp.exp(decay) * far[:depth], near[depth:] + far[depth:]]
        )

    count = lax.axis_size("seq")
    covered = along(own, direction)
    distance = 2
    while distance < count:
        window = combine(own, covered)
        covered = combine(covered, along(window, direction * distance))
        distance *= 2
    return covered


def scatter_rows(keep, send):
    parts = lax.axis_size("head")
    both = keep + swap(send)
    rows = both.shape[0] // parts
    pieces = [both[part * rows : (part + 1) * rows] for part in range(parts)]
    return [pieces[0]] + [across(pieces[part], part) for part in range(1, parts)]


def collect_rows(piece):
    parts = lax.axis_size("head")
    own = jnp.concatenate([piece] + [across(piece, part) for part in range(1, parts)])
    return own, swap(own)


def on_device(
    inputs, cotangent, in_gain, w_z, w_x, w_bc, w_dt, dt_bias, a_log, skip, conv_x, conv_bc,
    convb_x, convb_bc, norm_gain, w_out
):
    section = lax.axis_index("section")
    head = lax.axis_index("head")
    parts = lax.axis_size("head")
    where = jnp.stack([section, head]).astype(jnp.int32)
    micro, tokens, model_w = inputs.shape
    inner = w_z.shape[2] // 2
    heads_n = w_dt.shape[2] // 2
    state_loc = w_bc.shape[3]
    state_w = state_loc * parts
    channels = inner + 2 * state_w
    rows = tokens // (2 * parts)
    mine = section == 0

    def other_half(whole, axis):
        size = whole.shape[axis] // 2
        return lax.dynamic_slice_in_dim(whole, (1 - section) * size, size, axis).astype(F32)

    def share(whole, axis):
        size = whole.shape[axis] // 2
        own = lax.dynamic_slice_in_dim(whole, section * size, size, axis)
        got = swap(other_half(whole, axis))
        return jnp.where(mine, own, got), jnp.where(mine, got, own)

    pack = jnp.concatenate([w_bc[0].astype(F32), conv_bc[0], convb_bc], axis=0)
    pack = pack.reshape(model_w + CONV + 1, 2 * state_loc)
    pack = jnp.concatenate([pack, jnp.zeros((EDGE - CONV - 1, 2 * state_loc), F32)], axis=0)
    gathered = [pack] + [across(pack, part) for part in range(1, parts)]
    narrow = jnp.pad(w_dt[0].astype(F32), ((0, EDGE), (0, LANES - 2 * heads_n)))
    own_pack = jnp.concatenate(
        [one[:, :state_loc] for one in gathered]
        + [one[:, state_loc:] for one in gathered]
        + [narrow],
        axis=1,
    )
    other_pack = swap(own_pack)
    got_zx = swap(jnp.concatenate([other_half(w_z[0], 1), other_half(w_x[0], 1)], axis=1))
    got_out = swap(other_half(w_out[0], 0))
    picked = kernel_call(
        functools.partial(pick_weights, heads_n=heads_n),
        [((model_w, 2 * inner), BF16)] * 2
        + [((model_w, 2 * state_w), BF16)] * 2
        + [((model_w, LANES), BF16)] * 2
        + [((inner, model_w), BF16)] * 2,
        (where, w_z[0], w_x[0], w_out[0], got_zx, got_out, own_pack, other_pack),
        4,
    )
    w_zxs, w_bcs, w_dts, w_outs = (picked[2 * at : 2 * at + 2] for at in range(4))
    own_rows = own_pack[model_w:, : 2 * state_w]
    other_rows = other_pack[model_w:, : 2 * state_w]
    pack_rows = (jnp.where(mine, own_rows, other_rows), jnp.where(mine, other_rows, own_rows))
    conv_xs = share(jnp.concatenate([conv_x[0], convb_x, norm_gain], axis=0), 1)
    head_rows = share(jnp.concatenate([dt_bias, a_log, skip], axis=0), 1)
    head_rows = [jnp.pad(one, ((0, EDGE - 3), (0, LANES - heads_n))) for one in head_rows]
    other_gain = swap(in_gain)
    in_gains = (jnp.where(mine, in_gain, other_gain), jnp.where(mine, other_gain, in_gain))
    taps = []
    gains = []
    for conv_part, pack_part in zip(conv_xs, pack_rows):
        five = jnp.concatenate([conv_part[: CONV + 1], pack_part[: CONV + 1]], axis=1)
        taps.append(jnp.pad(five, ((0, EDGE - CONV - 1), (0, 0))))
        gains.append(conv_part[CONV + 1 : CONV + 2])

    start = (section * parts + head) * rows
    chunk_in = lax.dynamic_slice_in_dim(inputs, start, rows, 1).astype(F32)
    chunk_cot = lax.dynamic_slice_in_dim(cotangent, start, rows, 1).astype(F32)
    halo_in = along(inputs[:, tokens - EDGE :].astype(F32), 1)

    project_outs = [
        ((tokens, model_w), BF16),
        ((tokens, inner), F32),
        ((tokens + EDGE, channels), F32),
        ((tokens, channels), F32),
        ((tokens, LANES), F32),
        ((tokens, LANES), F32),
        ((tokens, inner), F32),
        ((state_w + EDGE, inner), F32),
    ]
    half_rows = tokens // 2

    def summed(sums):
        sums = sums + swap(sums)
        got = [across(sums, part) for part in range(1, parts)]
        return functools.reduce(jnp.add, got, sums)

    def forward_first(index):
        normed, gate, pad, conv, dt_val, cum, local, state = kernel_call(
            first_forward, project_outs,
            (inputs[index], halo_in[index], in_gains[0], w_zxs[0], w_bcs[0], w_dts[0], taps[0],
             head_rows[0]),
            5, scalars=False,
        )
        entry = carried(state, 1)
        ssd, sums = kernel_call(
            first_output, [((tokens, inner), F32), ((EDGE, tokens), F32)],
            (local, entry, conv, cum, gate), 2, scalars=False,
        )
        sums = summed(sums)
        norm_out, keep, send = kernel_call(
            functools.partial(first_branch, parts),
            [((tokens, inner), BF16), ((half_rows, model_w), F32), ((half_rows, model_w), F32)],
            (where, sums, ssd, gate, gains[0], w_outs[0]),
            2, scratch=[pltpu.VMEM((tokens, model_w), F32)],
        )
        (chunk,) = kernel_call(
            add_plain, [((rows, model_w), F32)], (chunk_in[index], *scatter_rows(keep, send)), 1,
            scalars=False,
        )
        own, other = collect_rows(chunk)
        kept = (normed, gate, pad, conv, dt_val, cum, state, entry, ssd)
        return kept, chunk, own, other, sums

    def forward_second(index, own, other):
        top = jnp.where(mine, other, own)
        at = jnp.bitwise_xor(head, parts - 1) * rows + rows - EDGE
        halo = along(lax.dynamic_slice_in_dim(top, at, EDGE, 0), 1)
        block_in, normed, gate, pad, conv, dt_val, cum, local, state = kernel_call(
            functools.partial(later_forward, parts),
            [((tokens, model_w), F32)] + project_outs,
            (where, own, other, halo, in_gains[1], w_zxs[1], w_bcs[1], w_dts[1], taps[1],
             head_rows[1]),
            5,
        )
        entry = carried(state, 1)
        ssd, grad_norm, sums = kernel_call(
            second_output,
            [((tokens, inner), F32), ((tokens, inner), F32), ((EDGE, tokens), F32)],
            (local, entry, conv, cum, gate, gains[1], w_outs[1], cotangent[index]),
            3, scalars=False,
        )
        sums = summed(sums)
        kept = (normed, gate, pad, conv, dt_val, cum, state, entry, ssd)
        return kept, block_in, grad_norm, sums

    gate_outs = [
        ((tokens, inner), F32),
        ((tokens, inner), BF16),
        ((tokens, inner), BF16),
        ((EDGE, inner), F32),
        ((state_w + EDGE, inner), F32),
    ]

    def back_rest(block, kept, dy, dz, grad_entry, block_in):
        normed, gate, pad, conv, dt_val, cum, state, entry, ssd = kept
        later = carried(grad_entry, -1)
        mixed, ddt, small, head_sums = kernel_call(
            scan_back,
            [((tokens + EDGE, channels), F32), ((tokens, LANES), BF16), ((EDGE, channels), F32),
             ((EDGE, LANES), F32)],
            (dy, ssd, conv, pad, dt_val, cum, entry, state, later, taps[block], head_rows[block]),
            9, scratch=[pltpu.VMEM((tokens + 3 * EDGE, channels), F32)], scalars=False,
        )
        from_next = along(mixed[:EDGE], -1)
        x_low, grad_bc, gain_sum, keep, send = kernel_call(
            functools.partial(normed_back, parts),
            [((tokens, inner), BF16), ((tokens, 2 * state_w), F32), ((EDGE, model_w), F32),
             ((half_rows, model_w), F32), ((half_rows, model_w), F32)],
            (where, mixed, from_next, dz, ddt, w_zxs[block], w_bcs[block], w_dts[block], block_in),
            4, scratch=[pltpu.VMEM((tokens, model_w), F32)],
        )
        return x_low, ddt, grad_bc, small, head_sums, gain_sum, keep, send

    def input_grad(block, grad_chunk, in_chunk, keep, send):
        (chunk,) = kernel_call(
            input_back, [((rows, model_w), F32)],
            (grad_chunk, in_chunk, in_gains[block], *scatter_rows(keep, send)), 1, scalars=False,
        )
        return chunk

    def weight_grads(normed_all, dz_all, norm_all, grad_all, rest_all, grow_all):
        def over_tokens(lefts, rights):
            return functools.reduce(
                jnp.add, [dot_low(a, b, TN) for a, b in zip(lefts, rights)]
            )

        def total(values):
            return functools.reduce(jnp.add, values)

        x_low, ddt, grad_bc, small, head_sums, gain_sum = zip(*[one[:6] for one in rest_all])
        g_w_out = lax.psum_scatter(
            over_tokens(norm_all, grad_all), "seq", scatter_dimension=1, tiled=True
        )
        g_w_z = lax.psum_scatter(
            over_tokens(normed_all, dz_all), "seq", scatter_dimension=0, tiled=True
        )
        g_w_x = lax.psum_scatter(
            over_tokens(normed_all, x_low), "seq", scatter_dimension=0, tiled=True
        )
        kept_bc = jnp.where(mine, grad_bc[0], grad_bc[1])
        sent_bc = jnp.where(mine, grad_bc[1], grad_bc[0])
        small_bc = total([one[:, inner:] for one in small])
        own_bc = jnp.concatenate([kept_bc + swap(sent_bc), small_bc], axis=0)

        def part_of(part):
            low = part * state_loc
            return jnp.concatenate(
                [own_bc[:, low : low + state_loc],
                 own_bc[:, state_w + low : state_w + low + state_loc]], axis=1
            )

        sum_bc = functools.reduce(
            jnp.add, [across(part_of(part), part) for part in range(1, parts)], part_of(0)
        )
        bc_low = sum_bc[:tokens].astype(BF16)
        normed_own = jnp.where(mine, normed_all[0], normed_all[1])
        g_narrow = jnp.concatenate(
            [dot_low(normed_own, bc_low, TN), over_tokens(normed_all, ddt)[:, :heads_n]], axis=1
        )
        g_narrow = lax.psum_scatter(g_narrow, "seq", scatter_dimension=0, tiled=True)
        grow = total([one[:1] for one in grow_all])
        gain = total([one[:1] for one in gain_sum])
        row_set = lax.psum(
            (
                total([one[:, :inner] for one in small]),
                sum_bc[tokens:],
                grow,
                total(head_sums),
            ),
            "seq",
        )
        gain = lax.psum(gain, ("section", "seq", "head"))
        return g_w_z, g_w_x, g_w_out, g_narrow, row_set, gain

    firsts = [forward_first(index) for index in range(micro)]
    seconds = [forward_second(index, firsts[index][2], firsts[index][3]) for index in range(micro)]

    gates = []
    rests = []
    grads = []
    for index in range(micro):
        kept, block_in, grad_norm, sums = seconds[index]
        gates.append(
            kernel_call(
                second_gate, gate_outs,
                (sums, grad_norm, kept[8], kept[1], gains[1], kept[3], kept[5], kept[6]),
                4, scalars=False,
            )
        )
    for index in range(micro):
        kept, block_in = seconds[index][:2]
        dy, dz, norm_out, grow, grad_entry = gates[index]
        rest = back_rest(1, kept, dy, dz, grad_entry, block_in)
        rests.append(rest)
        grads.append(
            input_grad(1, chunk_cot[index], firsts[index][1], rest[6], rest[7])
        )
    upper = []
    for index in range(micro):
        keep, send = kernel_call(
            functools.partial(out_project, parts),
            [((half_rows, model_w), F32), ((half_rows, model_w), F32)],
            (where, gates[index][2], w_outs[1]),
            2, scratch=[pltpu.VMEM((tokens, model_w), F32)],
        )
        (chunk,) = kernel_call(
            add_plain, [((rows, model_w), F32)], (firsts[index][1], *scatter_rows(keep, send)), 1,
            scalars=False,
        )
        upper.extend(collect_rows(chunk))
    top_set = weight_grads(
        [one[0][0] for one in seconds], [one[1] for one in gates], [one[2] for one in gates],
        [cotangent[index] for index in range(micro)], rests, [one[3] for one in gates],
    )

    gates = []
    rests = []
    lows = []
    lower = []
    for index in range(micro):
        own, other = collect_rows(grads[index])
        kept = firsts[index][0]
        block_in = seconds[index][1]
        sums = firsts[index][4]
        low, *gate_set = kernel_call(
            functools.partial(first_gate, parts), [((tokens, model_w), BF16)] + gate_outs,
            (where, own, other, block_in, inputs[index], sums, w_outs[0], kept[8], kept[1],
             gains[0], kept[3], kept[5], kept[6]),
            5, scratch=[pltpu.VMEM((tokens, model_w), F32)],
        )
        lows.append(low)
        gates.append(gate_set)
    for index in range(micro):
        kept = firsts[index][0]
        dy, dz, norm_out, grow, grad_entry = gates[index]
        rest = back_rest(0, kept, dy, dz, grad_entry, inputs[index])
        rests.append(rest)
        chunk = input_grad(0, grads[index], chunk_in[index], rest[6], rest[7])
        lower.extend(collect_rows(chunk))
    low_set = weight_grads(
        [one[0][0] for one in firsts], [one[1] for one in gates], [one[2] for one in gates],
        lows, rests, [one[3] for one in gates],
    )

    (ends,) = kernel_call(
        functools.partial(lay_out, parts), [((micro, tokens, model_w), F32)],
        (where, *lower, *upper), 2,
    )

    def own_block(index):
        return jnp.where(mine, low_set[index], top_set[index])

    def whole_of(index, axis):
        own = own_block(index)
        got = swap(jnp.where(mine, top_set[index], low_set[index]))
        return jnp.concatenate(
            [jnp.where(mine, own, got), jnp.where(mine, got, own)], axis=axis
        )

    g_w_z = whole_of(0, 1)
    g_w_x = whole_of(1, 1)
    g_w_out = whole_of(2, 0)
    own_narrow = own_block(3)
    got_narrow = swap(jnp.where(mine, top_set[3], low_set[3]))
    g_w_bc = (own_narrow + got_narrow)[:, : 2 * state_loc].reshape(-1, 2, state_loc)
    own_dt = own_narrow[:, 2 * state_loc :]
    got_dt = got_narrow[:, 2 * state_loc :]
    g_w_dt = jnp.concatenate(
        [jnp.where(mine, own_dt, got_dt), jnp.where(mine, got_dt, own_dt)], axis=1
    )
    low_rows, top_rows = low_set[4], top_set[4]
    bc_rows = [jnp.where(mine, low_rows[1], top_rows[1]), jnp.where(mine, top_rows[1], low_rows[1])]
    bc_rows = bc_rows[0] + swap(bc_rows[1])

    def widened(low_one, top_one):
        own = jnp.where(mine, low_one, top_one)
        got = swap(jnp.where(mine, top_one, low_one))
        return jnp.concatenate([jnp.where(mine, own, got), jnp.where(mine, got, own)], axis=1)

    x_rows = widened(low_rows[0], top_rows[0])
    g_norm_gain = widened(low_rows[2], top_rows[2])
    head_set = widened(low_rows[3][:, :heads_n], top_rows[3][:, :heads_n])
    g_in_gain = jnp.where(mine, low_set[5], top_set[5])
    return (
        ends[None],
        g_in_gain,
        g_w_z[None],
        g_w_x[None],
        g_w_bc[None],
        g_w_dt[None],
        head_set[0:1],
        head_set[1:2],
        head_set[2:3],
        x_rows[None, :CONV],
        bc_rows[:CONV].reshape(1, CONV, 2, state_loc),
        x_rows[CONV : CONV + 1],
        bc_rows[CONV : CONV + 1].reshape(1, 2, state_loc),
        g_norm_gain,
        g_w_out[None],
    )


def solution(mesh):
    in_specs = (
        P(None, "seq", None),
        P(None, "seq", None),
        P("section", None),
        P("section", None, "head"),
        P("section", None, "head"),
        P("section", None, None, "head"),
        P("section", None, "head"),
        P("section", "head"),
        P("section", "head"),
        P("section", "head"),
        P("section", None, "head"),
        P("section", None, None, "head"),
        P("section", "head"),
        P("section", None, "head"),
        P("section", "head"),
        P("section", "head", None),
    )
    out_specs = (
        P("section", None, "seq", None),
        P("section", None),
        P("section", "seq", "head"),
        P("section", "seq", "head"),
        P("section", "seq", None, "head"),
        P("section", "seq", "head"),
        P("section", "head"),
        P("section", "head"),
        P("section", "head"),
        P("section", None, "head"),
        P("section", None, None, "head"),
        P("section", "head"),
        P("section", None, "head"),
        P("section", "head"),
        P("section", "head", "seq"),
    )
    return jax.shard_map(
        on_device, mesh=mesh, in_specs=in_specs, out_specs=out_specs, check_vma=False
    )
```

time: 1420 us -> 546 us (0.38)
  waiting for transfers between devices: 565 us -> 127 us
  matrix products: 225 us -> 16.7 us
  local copies, waits for them, and re-layouts: 236 us -> 52.2 us
  other arithmetic: 204 us -> 43.5 us
  starting transfers between devices: 26.9 us -> 160 us
  blocking collectives: 125 us -> 59.8 us
  Pallas kernels: 0 us -> 58.6 us
    psum x5 -> x0, waiting for transfers between devices: 256 us -> none  [the longest x3 153 us: forward_block(): branch = lax.psum(matmul_low(norm_out, w_out), 'head')]
    dot_general x141 -> x18, matrix products: 225 us -> 16.7 us  [dot_low(): lax.dot_general(left.astype(BF16), right.astype(BF16), dims, preferred_el...]
    ppermute x10 -> x128, starting transfers between devices: 26.1 us -> 160 us  [the longest x69 88.6 us: across(): return lax.ppermute(block, 'head', [(i, i ^ mask) for i in range(count)])]
    reduce_scatter x5 -> x8, waiting for transfers between devices: 154 us -> 32.6 us  [the longest x2 32.5 us: weight_grads(): lax.psum_scatter(over_tokens(normed_all, x_low), 'seq', scatter_dimension...]
    unnamed x22 -> x8, waiting for transfers between devices: 92.3 us -> 0.13 us
    ppermute x10 -> x128, waiting for transfers between devices: 13.7 us -> 94.3 us  [the longest x69 48.6 us: across(): return lax.ppermute(block, 'head', [(i, i ^ mask) for i in range(count)])]
    another operation x52 -> x1, other arithmetic: 63 us -> 0.58 us  [on_device(): where = jnp.stack([section, head]).astype(jnp.int32)]
    pallas_call x0 -> x34, Pallas kernels: none -> 58.6 us  [kernel_call(): pl.pallas_call(body, out_shape=[jax.ShapeDtypeStruct(shape, dtype) for sh...]
  transfers between devices with their start and end apart: 29 -> 136, of which waited for: 21 -> 49; matrix products, arithmetic and copies ran while one was open for 20% -> 16% of each run, Pallas kernels for 0% -> 10%
where the time goes in v1:
time: 546 us; the launch traced here: 536 us
  starting transfers between devices  160 us (29%)
  waiting for transfers between devices  127 us (23%)
  blocking collectives  59.8 us (11%)
  Pallas kernels  58.6 us (11%)
  local copies, waits for them, and re-layouts  52.2 us (10%)
  other arithmetic  43.5 us (8%)
  between operations  17.9 us (3%)
  matrix products  16.7 us (3%)
    ppermute x69, starting transfers between devices, across(): return lax.ppermute(block, 'head', [(i, i ^ mask) for i in range(count)])  88.6 us
    ppermute x23, starting transfers between devices, along(): lax.ppermute(block, 'seq', [(i, i + distance) for i in devices if i + dis...  65.3 us
    pallas_call x34, Pallas kernels, kernel_call(): pl.pallas_call(body, out_shape=[jax.ShapeDtypeStruct(shape, dtype) for sh...  58.6 us
    ppermute x69, waiting for transfers between devices, across(): return lax.ppermute(block, 'head', [(i, i ^ mask) for i in range(count)])  48.6 us
    ppermute x23, waiting for transfers between devices, along(): lax.ppermute(block, 'seq', [(i, i + distance) for i in devices if i + dis...  42.8 us
    psum x1, blocking collectives, weight_grads(): gain = lax.psum(gain, ('section', 'seq', 'head'))  40.9 us
    reduce_scatter x2, waiting for transfers between devices, weight_grads(): lax.psum_scatter(over_tokens(normed_all, x_low), 'seq', scatter_dimension...  32.5 us
    unnamed x348, local copies, waits for them, and re-layouts  30.9 us
  transfers between devices with their start and end apart: 136, of which 49 were waited for; matrix products, arithmetic and copies ran while one was open for 16% of the time, Pallas kernels for 10%

profile of v1, /device:TPU:0, one launch (start us, length us, event | category | flops | bytes accessed | tf_op | source)
XLA Modules:
  0.0 536.0 jit_solution(10372135801593337846)
XLA Ops:
  11.1 2.9 collective-permute-start.4
  16.4 4.6 collective-permute-start
  26.5 2.7 collective-permute-done.5
  36.3 3.9 concatenate.170.own_pack_ref
  48.7 3.5 concatenate.172
  59.4 3.4 shard_map.271
  62.9 2.6 shard_map.272
  67.0 3.5 collective-permute-start.10
  70.5 2.6 shard_map.286
  73.2 3.5 collective-permute-start.53
  76.8 2.9 collective-permute-start.11
  79.8 9.5 %collective-permute-start.54 = (f32[136,256]{1,0:T(8,128)S(1)}, f32[136,256]{1,0:T(8,128)S(1)}, u32[]{:S(2)}, u32[]{:S(2)}) collective-permute-start(f32[136,256]{1,0:T(8,128)S(1)} %pad_maximum_fusion.18), channel_id=1, source_target_pairs={{0,8},{4,12},{1,9},{5,13},{2,10},{6,14},{3,11},{7,15},{16,24},{20,... | collective-permute-start | bytes 417800 | tf_op jit(solution)/shard_map/ppermute | solution.py:503
  99.9 2.9 collective-permute-start.58
  122.3 2.4 collective-permute-start.22
  128.0 4.8 collective-permute-start.65
  134.5 2.8 collective-permute-done.65
  146.3 5.8 %collective-permute-start.67 = (f32[8,1024]{1,0:T(8,128)S(1)}, f32[8,1024]{1,0:T(8,128)S(1)}, u32[]{:S(2)}, u32[]{:S(2)}) collective-permute-start(f32[8,1024]{1,0:T(8,128)S(1)} %dynamic-slice_select_fusion), channel_id=1, source_target_pairs={{0,4},{4,8},{8,12},{1,5},{5,9},{9,13},{2,6},{6,10},{10,14},{3,7},{... | collective-permute-start | bytes 98312 | tf_op jit(solution)/shard_map/ppermute | solution.py:503
  152.1 3.9 shard_map.276
  156.0 3.4 collective-permute-start.25
  159.4 3.9 shard_map.290
  165.4 2.5 collective-permute-start.26
  169.4 9.6 %collective-permute-start.69 = (f32[136,256]{1,0:T(8,128)S(1)}, f32[136,256]{1,0:T(8,128)S(1)}, u32[]{:S(2)}, u32[]{:S(2)}) collective-permute-start(f32[136,256]{1,0:T(8,128)S(1)} %pad_maximum_fusion.20), channel_id=1, source_target_pairs={{0,8},{4,12},{1,9},{5,13},{2,10},{6,14},{3,11},{7,15},{16,24},{20,... | collective-permute-start | bytes 417800 | tf_op jit(solution)/shard_map/ppermute | solution.py:503
  194.1 4.3 collective-permute-done.31
  201.8 10.4 %collective-permute-done.32 = f32[136,256]{1,0:T(8,128)S(1)} collective-permute-done((f32[136,256]{1,0:T(8,128)S(1)}, f32[136,256]{1,0:T(8,128)S(1)}, u32[]{:S(2)}, u32[]{:S(2)}) %collective-permute-start.32) | collective-permute-done | bytes 139296 | tf_op jit(solution)/shard_map/ppermute | solution.py:503
  212.3 4.0 shard_map.279
  217.7 3.9 shard_map.293
  225.3 2.6 collective-permute-done.76.next_ref
  244.9 2.5 collective-permute-done.79.refs_1_
  247.5 3.4 collective-permute-start.121
  252.1 3.0 collective-permute-start.83
  257.1 2.4 collective-permute-done.120
  273.9 2.4 shard_map.282
  283.0 2.8 collective-permute-done.42
  287.2 3.4 collective-permute-done.85
  292.1 9.1 %collective-permute-done.43 = f32[136,256]{1,0:T(8,128)S(1)} collective-permute-done((f32[136,256]{1,0:T(8,128)S(1)}, f32[136,256]{1,0:T(8,128)S(1)}, u32[]{:S(2)}, u32[]{:S(2)}) %collective-permute-start.43) | collective-permute-done | bytes 139296 | tf_op jit(solution)/shard_map/ppermute | solution.py:503
  301.4 4.0 shard_map.283
  307.0 4.0 shard_map.297
  312.5 4.7 collective-permute-done.87.next_ref
  328.6 3.3 collective-permute-done.117
  340.5 2.4 convolution_add_fusion
  373.2 3.1 collective-permute-start.110
  378.4 2.5 collective-permute-done.110
  384.8 40.9 %all-reduce.6 = (f32[1,1024]{1,0:T(1,128)S(1)}, f32[1,1024]{1,0:T(1,128)S(1)}) all-reduce(f32[1,1024]{1,0:T(1,128)S(1)} %slice_add_fusion.24, f32[1,1024]{1,0:T(1,128)S(1)} %slice_add_fusion.23), channel_id=1, replica_groups=mesh['section'=2,'seq'=4,'head'=4] {'section','seq','head'}, use_global_device_ids=true, to_apply=%region_0.1 | all-reduce | flops 2048 | bytes 16384 | tf_op jit(solution)/shard_map/psum | solution.py:764
  428.1 18.9 %all-reduce.7 = (f32[8,128]{1,0:T(8,128)S(1)}, f32[8,128]{1,0:T(8,128)S(1)}, f32[8,256]{1,0:T(8,128)S(1)}, f32[8,256]{1,0:T(8,128)S(1)}, f32[8,64]{1,0:T(8,128)S...) all-reduce(f32[8,128]{1,0:T(8,128)S(1)} %add.416, ...), channel_id=1, replica_groups=mesh['section'=2,'seq'=4,'head'=4] {'seq'}, use_global_device_ids=true, to_apply=%region_9.10 | all-reduce | flops 7680 | bytes 61440 | tf_op jit(solution)/shard_map/psum | solution.py:755
  469.0 2.9 collective-permute-done.90.refs_1_
  487.3 2.8 shard_map.304
  492.3 4.3 reduce-scatter.15.cloned.1.call-done
  496.6 28.2 %reduce-scatter.13.cloned.1.call-done = f32[256,256]{1,0:T(8,128)} async-done(((f32[1024,256]{1,0:T(8,128)}), f32[256,256]{1,0:T(8,128)}) %reduce-scatter.13.cloned.1.call-update) | async-done | bytes 262160 | tf_op jit(solution)/shard_map/reduce_scatter | solution.py:729
  (838 shorter events, 254.1 us)
Async XLA Ops:
  7.2 469.7 %reduce-scatter.19.cloned.1.call-start = ((), (), s32[]{:S(2)}) async-start(), calls=%async_computation.13 | async-start | bytes 368640 | tf_op jit(solution)/shard_map/reduce_scatter | solution.py:752
  11.1 13.8 %collective-permute-start.4 = (f32[1032,64]{0,1:T(8,128)}, f32[1032,64]{0,1:T(8,128)}, u32[]{:S(2)}, u32[]{:S(2)}) collective-permute-start(f32[1032,64]{0,1:T(8,128)} %concatenate.169.clone), channel_id=1, source_target_pairs={{0,1},{1,0},{2,3},{3,2},{4,5},{5,4},{6,7},{7,6},{8,9},{9,8},{10,11... | collective-permute-start | bytes 792584 | tf_op jit(solution)/shard_map/ppermute | solution.py:498
  14.1 15.1 %collective-permute-start.5 = (f32[1032,64]{0,1:T(8,128)}, f32[1032,64]{0,1:T(8,128)}, u32[]{:S(2)}, u32[]{:S(2)}) collective-permute-start(f32[1032,64]{0,1:T(8,128)} %concatenate.169.clone), channel_id=1, source_target_pairs={{0,2},{1,3},{2,0},{3,1},{4,6},{5,7},{6,4},{7,5},{8,10},{9,11},{10,... | collective-permute-start | bytes 792584 | tf_op jit(solution)/shard_map/ppermute | solution.py:498
  15.6 14.6 %collective-permute-start.6 = (f32[1032,64]{0,1:T(8,128)}, f32[1032,64]{0,1:T(8,128)S(1)}, u32[]{:S(2)}, u32[]{:S(2)}) collective-permute-start(f32[1032,64]{0,1:T(8,128)} %concatenate.169.clone), channel_id=1, source_target_pairs={{0,3},{1,2},{2,1},{3,0},{4,7},{5,6},{6,5},{7,4},{8,11},{9,10},{10,... | collective-permute-start | bytes 792584 | tf_op jit(solution)/shard_map/ppermute | solution.py:498
  16.4 31.0 %collective-permute-start = (f32[2,8,1024]{2,1,0:T(8,128)S(1)}, f32[2,8,1024]{2,1,0:T(8,128)}, u32[]{:S(2)}, u32[]{:S(2)}) collective-permute-start(f32[2,8,1024]{2,1,0:T(8,128)S(1)} %slice_convert_fusion.4), channel_id=1, source_target_pairs={{0,4},{4,8},{8,12},{1,5},{5,9},{9,13},{2,6},{6,10},{10,14},{3,7},{... | collective-permute-start | bytes 196616 | tf_op jit(solution)/shard_map/ppermute | solution.py:503
  20.9 23.9 %collective-permute-start.1 = (f32[1,1024]{1,0:T(1,128)S(1)}, f32[1,1024]{1,0:T(1,128)S(1)}, u32[]{:S(2)}, u32[]{:S(2)}) collective-permute-start(f32[1,1024]{1,0:T(1,128)S(1)} %copy-done.164), channel_id=1, source_target_pairs={{0,16},{16,0},{1,17},{17,1},{2,18},{18,2},{3,19},{19,3},{4,20},{20... | collective-permute-start | bytes 12296 | tf_op jit(solution)/shard_map/ppermute | solution.py:493
  25.0 28.6 %collective-permute-start.2 = (f32[1024,512]{1,0:T(8,128)}, f32[1024,512]{1,0:T(8,128)}, u32[]{:S(2)}, u32[]{:S(2)}) collective-permute-start(f32[1024,512]{1,0:T(8,128)} %maximum_convert_fusion), channel_id=1, source_target_pairs={{0,16},{16,0},{1,17},{17,1},{2,18},{18,2},{3,19},{19,3},{4,20},{20... | collective-permute-start | bytes 6291464 | tf_op jit(solution)/shard_map/ppermute | solution.py:493
  29.2 14.3 %collective-permute-start.9 = (f32[3,4]{1,0:T(4,128)S(1)}, f32[3,4]{1,0:T(4,128)S(1)}, u32[]{:S(2)}, u32[]{:S(2)}) collective-permute-start(f32[3,4]{1,0:T(4,128)S(1)} %constant_dynamic-slice_fusion), channel_id=1, source_target_pairs={{0,16},{16,0},{1,17},{17,1},{2,18},{18,2},{3,19},{19,3},{4,20},{20... | collective-permute-start | bytes 152 | tf_op jit(solution)/shard_map/ppermute | solution.py:493
  40.3 12.0 %collective-permute-start.7 = (f32[1032,384]{1,0:T(8,128)S(1)}, f32[1032,384]{1,0:T(8,128)}, u32[]{:S(2)}, u32[]{:S(2)}) collective-permute-start(f32[1032,384]{1,0:T(8,128)S(1)} %concatenate.170.own_pack_ref), channel_id=1, source_target_pairs={{0,16},{16,0},{1,17},{17,1},{2,18},{18,2},{3,19},{19,3},{4,20},{20... | collective-permute-start | bytes 4755464 | tf_op jit(solution)/shard_map/ppermute | solution.py:493
  43.5 10.1 %collective-permute-start.3 = (f32[256,1024]{1,0:T(8,128)}, f32[256,1024]{1,0:T(8,128)}, u32[]{:S(2)}, u32[]{:S(2)}) collective-permute-start(f32[256,1024]{1,0:T(8,128)} %bitcast_convert_fusion), channel_id=1, source_target_pairs={{0,16},{16,0},{1,17},{17,1},{2,18},{18,2},{3,19},{19,3},{4,20},{20... | collective-permute-start | bytes 3145736 | tf_op jit(solution)/shard_map/ppermute | solution.py:493
  67.0 9.7 %collective-permute-start.10 = (f32[136,256]{1,0:T(8,128)S(1)}, f32[136,256]{1,0:T(8,128)S(1)}, u32[]{:S(2)}, u32[]{:S(2)}) collective-permute-start(f32[136,256]{1,0:T(8,128)S(1)} %get-tuple-element.137.state_ref), channel_id=1, source_target_pairs={{0,4},{4,8},{8,12},{1,5},{5,9},{9,13},{2,6},{6,10},{10,14},{3,7},{... | collective-permute-start | bytes 417800 | tf_op jit(solution)/shard_map/ppermute | solution.py:503
  76.8 12.6 %collective-permute-start.11 = (f32[136,256]{1,0:T(8,128)S(1)}, f32[136,256]{1,0:T(8,128)S(1)}, u32[]{:S(2)}, u32[]{:S(2)}) collective-permute-start(f32[136,256]{1,0:T(8,128)S(1)} %pad_maximum_fusion.10), channel_id=1, source_target_pairs={{0,8},{4,12},{1,9},{5,13},{2,10},{6,14},{3,11},{7,15},{16,24},{20,... | collective-permute-start | bytes 417800 | tf_op jit(solution)/shard_map/ppermute | solution.py:503
  79.8 11.9 %collective-permute-start.54 = (f32[136,256]{1,0:T(8,128)S(1)}, f32[136,256]{1,0:T(8,128)S(1)}, u32[]{:S(2)}, u32[]{:S(2)}) collective-permute-start(f32[136,256]{1,0:T(8,128)S(1)} %pad_maximum_fusion.18), channel_id=1, source_target_pairs={{0,8},{4,12},{1,9},{5,13},{2,10},{6,14},{3,11},{7,15},{16,24},{20,... | collective-permute-start | bytes 417800 | tf_op jit(solution)/shard_map/ppermute | solution.py:503
  99.9 10.9 %collective-permute-start.16 = (f32[128,1024]{1,0:T(8,128)}, f32[128,1024]{1,0:T(8,128)}, u32[]{:S(2)}, u32[]{:S(2)}) collective-permute-start(f32[128,1024]{1,0:T(8,128)} %get-tuple-element.145), channel_id=1, source_target_pairs={{0,16},{16,0},{1,17},{17,1},{2,18},{18,2},{3,19},{19,3},{4,20},{20... | collective-permute-start | bytes 1572872 | tf_op jit(solution)/shard_map/ppermute | solution.py:493
  122.3 10.5 %collective-permute-start.22 = (f32[32,1024]{1,0:T(8,128)S(1)}, f32[32,1024]{1,0:T(8,128)S(1)}, u32[]{:S(2)}, u32[]{:S(2)}) collective-permute-start(f32[32,1024]{1,0:T(8,128)S(1)} %shard_map.275.in_ref.base_ref), channel_id=1, source_target_pairs={{0,3},{1,2},{2,1},{3,0},{4,7},{5,6},{6,5},{7,4},{8,11},{9,10},{10,... | collective-permute-start | bytes 393224 | tf_op jit(solution)/shard_map/ppermute | solution.py:498
  146.3 13.1 %collective-permute-start.67 = (f32[8,1024]{1,0:T(8,128)S(1)}, f32[8,1024]{1,0:T(8,128)S(1)}, u32[]{:S(2)}, u32[]{:S(2)}) collective-permute-start(f32[8,1024]{1,0:T(8,128)S(1)} %dynamic-slice_select_fusion), channel_id=1, source_target_pairs={{0,4},{4,8},{8,12},{1,5},{5,9},{9,13},{2,6},{6,10},{10,14},{3,7},{... | collective-permute-start | bytes 98312 | tf_op jit(solution)/shard_map/ppermute | solution.py:503
  165.4 13.7 %collective-permute-start.26 = (f32[136,256]{1,0:T(8,128)S(1)}, f32[136,256]{1,0:T(8,128)S(1)}, u32[]{:S(2)}, u32[]{:S(2)}) collective-permute-start(f32[136,256]{1,0:T(8,128)S(1)} %pad_maximum_fusion.12), channel_id=1, source_target_pairs={{0,8},{4,12},{1,9},{5,13},{2,10},{6,14},{3,11},{7,15},{16,24},{20,... | collective-permute-start | bytes 417800 | tf_op jit(solution)/shard_map/ppermute | solution.py:503
  169.4 11.8 %collective-permute-start.69 = (f32[136,256]{1,0:T(8,128)S(1)}, f32[136,256]{1,0:T(8,128)S(1)}, u32[]{:S(2)}, u32[]{:S(2)}) collective-permute-start(f32[136,256]{1,0:T(8,128)S(1)} %pad_maximum_fusion.20), channel_id=1, source_target_pairs={{0,8},{4,12},{1,9},{5,13},{2,10},{6,14},{3,11},{7,15},{16,24},{20,... | collective-permute-start | bytes 417800 | tf_op jit(solution)/shard_map/ppermute | solution.py:503
  198.5 13.8 %collective-permute-start.32 = (f32[136,256]{1,0:T(8,128)S(1)}, f32[136,256]{1,0:T(8,128)S(1)}, u32[]{:S(2)}, u32[]{:S(2)}) collective-permute-start(f32[136,256]{1,0:T(8,128)S(1)} %pad_maximum_fusion.14), channel_id=1, source_target_pairs={{8,0},{12,4},{9,1},{13,5},{10,2},{14,6},{11,3},{15,7},{24,16},{28,... | collective-permute-start | bytes 417800 | tf_op jit(solution)/shard_map/ppermute | solution.py:503
  200.5 17.1 %collective-permute-start.75 = (f32[136,256]{1,0:T(8,128)S(1)}, f32[136,256]{1,0:T(8,128)S(1)}, u32[]{:S(2)}, u32[]{:S(2)}) collective-permute-start(f32[136,256]{1,0:T(8,128)S(1)} %pad_maximum_fusion.22), channel_id=1, source_target_pairs={{8,0},{12,4},{9,1},{13,5},{10,2},{14,6},{11,3},{15,7},{24,16},{28,... | collective-permute-start | bytes 417800 | tf_op jit(solution)/shard_map/ppermute | solution.py:503
  236.1 11.3 %collective-permute-start.79 = (f32[32,1024]{1,0:T(8,128)S(1)}, f32[32,1024]{1,0:T(8,128)S(1)}, u32[]{:S(2)}, u32[]{:S(2)}) collective-permute-start(f32[32,1024]{1,0:T(8,128)S(1)} %get-tuple-element.286), channel_id=1, source_target_pairs={{0,2},{1,3},{2,0},{3,1},{4,6},{5,7},{6,4},{7,5},{8,10},{9,11},{10,... | collective-permute-start | bytes 393224 | tf_op jit(solution)/shard_map/ppermute | solution.py:498
  237.7 13.2 %collective-permute-start.80 = (f32[32,1024]{1,0:T(8,128)S(1)}, f32[32,1024]{1,0:T(8,128)S(1)}, u32[]{:S(2)}, u32[]{:S(2)}) collective-permute-start(f32[32,1024]{1,0:T(8,128)S(1)} %get-tuple-element.285), channel_id=1, source_target_pairs={{0,3},{1,2},{2,1},{3,0},{4,7},{5,6},{6,5},{7,4},{8,11},{9,10},{10,... | collective-permute-start | bytes 393224 | tf_op jit(solution)/shard_map/ppermute | solution.py:498
  241.2 9.9 %collective-permute-start.40 = (f32[32,1024]{1,0:T(8,128)S(1)}, f32[32,1024]{1,0:T(8,128)S(1)}, u32[]{:S(2)}, u32[]{:S(2)}) collective-permute-start(f32[32,1024]{1,0:T(8,128)S(1)} %shard_map.281.grad_ref), channel_id=1, source_target_pairs={{0,3},{1,2},{2,1},{3,0},{4,7},{5,6},{6,5},{7,4},{8,11},{9,10},{10,... | collective-permute-start | bytes 393224 | tf_op jit(solution)/shard_map/ppermute | solution.py:498
  243.9 11.3 %collective-permute-start.38 = (f32[32,1024]{1,0:T(8,128)S(1)}, f32[32,1024]{1,0:T(8,128)S(1)}, u32[]{:S(2)}, u32[]{:S(2)}) collective-permute-start(f32[32,1024]{1,0:T(8,128)S(1)} %shard_map.281.grad_ref), channel_id=1, source_target_pairs={{0,1},{1,0},{2,3},{3,2},{4,5},{5,4},{6,7},{7,6},{8,9},{9,8},{10,11... | collective-permute-start | bytes 393224 | tf_op jit(solution)/shard_map/ppermute | solution.py:498
  247.5 9.5 %collective-permute-start.121 = (f32[264,64]{1,0:T(8,128)S(1)}, f32[264,64]{1,0:T(8,128)S(1)}, u32[]{:S(2)}, u32[]{:S(2)}) collective-permute-start(f32[264,64]{1,0:T(8,128)S(1)} %fusion.20), channel_id=1, source_target_pairs={{0,3},{1,2},{2,1},{3,0},{4,7},{5,6},{6,5},{7,4},{8,11},{9,10},{10,... | collective-permute-start | bytes 202760 | tf_op jit(solution)/shard_map/ppermute | solution.py:498
  252.1 9.6 %collective-permute-start.83 = (f32[32,1024]{1,0:T(8,128)S(1)}, f32[32,1024]{1,0:T(8,128)S(1)}, u32[]{:S(2)}, u32[]{:S(2)}) collective-permute-start(f32[32,1024]{1,0:T(8,128)S(1)} %shard_map.295.grad_ref), channel_id=1, source_target_pairs={{0,3},{1,2},{2,1},{3,0},{4,7},{5,6},{6,5},{7,4},{8,11},{9,10},{10,... | collective-permute-start | bytes 393224 | tf_op jit(solution)/shard_map/ppermute | solution.py:498
  263.6 14.9 %collective-permute-start.84 = (f32[128,1024]{1,0:T(8,128)}, f32[128,1024]{1,0:T(8,128)}, u32[]{:S(2)}, u32[]{:S(2)}) collective-permute-start(f32[128,1024]{1,0:T(8,128)} %pad_maximum_fusion.4.own_ref), channel_id=1, source_target_pairs={{0,16},{16,0},{1,17},{17,1},{2,18},{18,2},{3,19},{19,3},{4,20},{20... | collective-permute-start | bytes 1572872 | tf_op jit(solution)/shard_map/ppermute | solution.py:493
  264.7 212.2 %reduce-scatter.17.cloned.1.call-start = ((), (), s32[]{:S(2)}) async-start(), calls=%async_computation.12 | async-start | bytes 368640 | tf_op jit(solution)/shard_map/reduce_scatter | solution.py:752
  285.9 15.4 %collective-permute-start.43 = (f32[136,256]{1,0:T(8,128)S(1)}, f32[136,256]{1,0:T(8,128)S(1)}, u32[]{:S(2)}, u32[]{:S(2)}) collective-permute-start(f32[136,256]{1,0:T(8,128)S(1)} %pad_maximum_fusion.16), channel_id=1, source_target_pairs={{8,0},{12,4},{9,1},{13,5},{10,2},{14,6},{11,3},{15,7},{24,16},{28,... | collective-permute-start | bytes 417800 | tf_op jit(solution)/shard_map/ppermute | solution.py:503
  290.7 16.2 %collective-permute-start.86 = (f32[136,256]{1,0:T(8,128)S(1)}, f32[136,256]{1,0:T(8,128)S(1)}, u32[]{:S(2)}, u32[]{:S(2)}) collective-permute-start(f32[136,256]{1,0:T(8,128)S(1)} %pad_maximum_fusion.24), channel_id=1, source_target_pairs={{8,0},{12,4},{9,1},{13,5},{10,2},{14,6},{11,3},{15,7},{24,16},{28,... | collective-permute-start | bytes 417800 | tf_op jit(solution)/shard_map/ppermute | solution.py:503
  305.4 14.9 %collective-permute-start.44 = (f32[8,512]{1,0:T(8,128)S(1)}, f32[8,512]{1,0:T(8,128)S(1)}, u32[]{:S(2)}, u32[]{:S(2)}) collective-permute-start(f32[8,512]{1,0:T(8,128)S(1)} %slice.621), channel_id=1, source_target_pairs={{4,0},{8,4},{12,8},{5,1},{9,5},{13,9},{6,2},{10,6},{14,10},{7,3},{... | collective-permute-start | bytes 49160 | tf_op jit(solution)/shard_map/ppermute | solution.py:503
  335.5 149.0 %reduce-scatter.11.cloned.1.call-start = ((), (), s32[]{:S(2)}) async-start(), calls=%async_computation.9 | async-start | bytes 1310720 | tf_op jit(solution)/shard_map/reduce_scatter | solution.py:726
  337.3 147.2 %reduce-scatter.9.cloned.1.call-start = ((), (), s32[]{:S(2)}) async-start(), calls=%async_computation.8 | async-start | bytes 1310720 | tf_op jit(solution)/shard_map/reduce_scatter | solution.py:726
  339.1 151.0 %reduce-scatter.23.cloned.1.call-start = ((), (), s32[]{:S(2)}) async-start(), calls=%async_computation.15 | async-start | bytes 1310720 | tf_op jit(solution)/shard_map/reduce_scatter | solution.py:723
  343.0 147.1 %reduce-scatter.21.cloned.1.call-start = ((), (), s32[]{:S(2)}) async-start(), calls=%async_computation.14 | async-start | bytes 1310720 | tf_op jit(solution)/shard_map/reduce_scatter | solution.py:723
  345.8 150.8 %reduce-scatter.15.cloned.1.call-start = ((), (), s32[]{:S(2)}) async-start(), calls=%async_computation.11 | async-start | bytes 1310720 | tf_op jit(solution)/shard_map/reduce_scatter | solution.py:729
  355.1 169.7 %reduce-scatter.13.cloned.1.call-start = ((), (), s32[]{:S(2)}) async-start(), calls=%async_computation.10 | async-start | bytes 1310720 | tf_op jit(solution)/shard_map/reduce_scatter | solution.py:729
  362.6 10.5 %collective-permute-start.106 = (f32[32,1024]{1,0:T(8,128)S(1)}, f32[32,1024]{1,0:T(8,128)S(1)}, u32[]{:S(2)}, u32[]{:S(2)}) collective-permute-start(f32[32,1024]{1,0:T(8,128)S(1)} %get-tuple-element.274), channel_id=1, source_target_pairs={{0,2},{1,3},{2,0},{3,1},{4,6},{5,7},{6,4},{7,5},{8,10},{9,11},{10,... | collective-permute-start | bytes 393224 | tf_op jit(solution)/shard_map/ppermute | solution.py:498
  366.8 9.5 %collective-permute-start.102 = (f32[32,1024]{1,0:T(8,128)S(1)}, f32[32,1024]{1,0:T(8,128)S(1)}, u32[]{:S(2)}, u32[]{:S(2)}) collective-permute-start(f32[32,1024]{1,0:T(8,128)S(1)} %shard_map.301), channel_id=1, source_target_pairs={{0,3},{1,2},{2,1},{3,0},{4,7},{5,6},{6,5},{7,4},{8,11},{9,10},{10,... | collective-permute-start | bytes 393224 | tf_op jit(solution)/shard_map/ppermute | solution.py:498
  368.8 9.5 %collective-permute-start.101 = (f32[32,1024]{1,0:T(8,128)S(1)}, f32[32,1024]{1,0:T(8,128)S(1)}, u32[]{:S(2)}, u32[]{:S(2)}) collective-permute-start(f32[32,1024]{1,0:T(8,128)S(1)} %shard_map.301), channel_id=1, source_target_pairs={{0,2},{1,3},{2,0},{3,1},{4,6},{5,7},{6,4},{7,5},{8,10},{9,11},{10,... | collective-permute-start | bytes 393224 | tf_op jit(solution)/shard_map/ppermute | solution.py:498
  383.5 67.9 %collective-permute-start.45 = (f32[128,1024]{1,0:T(8,128)}, f32[128,1024]{1,0:T(8,128)S(1)}, u32[]{:S(2)}, u32[]{:S(2)}) collective-permute-start(f32[128,1024]{1,0:T(8,128)} %get-tuple-element.176), channel_id=1, source_target_pairs={{0,16},{16,0},{1,17},{17,1},{2,18},{18,2},{3,19},{19,3},{4,20},{20... | collective-permute-start | bytes 1572872 | tf_op jit(solution)/shard_map/ppermute | solution.py:493
  383.6 73.5 %collective-permute-start.88 = (f32[128,1024]{1,0:T(8,128)}, f32[128,1024]{1,0:T(8,128)}, u32[]{:S(2)}, u32[]{:S(2)}) collective-permute-start(f32[128,1024]{1,0:T(8,128)} %get-tuple-element.212), channel_id=1, source_target_pairs={{0,16},{16,0},{1,17},{17,1},{2,18},{18,2},{3,19},{19,3},{4,20},{20... | collective-permute-start | bytes 1572872 | tf_op jit(solution)/shard_map/ppermute | solution.py:493
  447.1 13.1 %collective-permute-start.124 = (f32[8,256]{1,0:T(8,128)S(1)}, f32[8,256]{1,0:T(8,128)S(1)}, u32[]{:S(2)}, u32[]{:S(2)}) collective-permute-start(f32[8,256]{1,0:T(8,128)S(1)} %broadcast_select_fusion.19), channel_id=1, source_target_pairs={{0,16},{16,0},{1,17},{17,1},{2,18},{18,2},{3,19},{19,3},{4,20},{20... | collective-permute-start | bytes 24584 | tf_op jit(solution)/shard_map/ppermute | solution.py:493
  460.2 11.7 %collective-permute-start.90 = (f32[32,1024]{1,0:T(8,128)S(1)}, f32[32,1024]{1,0:T(8,128)S(1)}, u32[]{:S(2)}, u32[]{:S(2)}) collective-permute-start(f32[32,1024]{1,0:T(8,128)S(1)} %get-tuple-element.282), channel_id=1, source_target_pairs={{0,2},{1,3},{2,0},{3,1},{4,6},{5,7},{6,4},{7,5},{8,10},{9,11},{10,... | collective-permute-start | bytes 393224 | tf_op jit(solution)/shard_map/ppermute | solution.py:498
  461.6 10.4 %collective-permute-start.91 = (f32[32,1024]{1,0:T(8,128)S(1)}, f32[32,1024]{1,0:T(8,128)S(1)}, u32[]{:S(2)}, u32[]{:S(2)}) collective-permute-start(f32[32,1024]{1,0:T(8,128)S(1)} %get-tuple-element.281), channel_id=1, source_target_pairs={{0,3},{1,2},{2,1},{3,0},{4,7},{5,6},{6,5},{7,4},{8,11},{9,10},{10,... | collective-permute-start | bytes 393224 | tf_op jit(solution)/shard_map/ppermute | solution.py:498
  471.9 15.3 %collective-permute-start.103 = (f32[128,1024]{1,0:T(8,128)S(1)}, f32[128,1024]{1,0:T(8,128)S(1)}, u32[]{:S(2)}, u32[]{:S(2)}) collective-permute-start(f32[128,1024]{1,0:T(8,128)S(1)} %pad_maximum_fusion.6.refs_4_), channel_id=1, source_target_pairs={{0,16},{16,0},{1,17},{17,1},{2,18},{18,2},{3,19},{19,3},{4,20},{20... | collective-permute-start | bytes 1572872 | tf_op jit(solution)/shard_map/ppermute | solution.py:493
  472.0 15.3 %collective-permute-start.111 = (f32[128,1024]{1,0:T(8,128)S(1)}, f32[128,1024]{1,0:T(8,128)S(1)}, u32[]{:S(2)}, u32[]{:S(2)}) collective-permute-start(f32[128,1024]{1,0:T(8,128)S(1)} %pad_maximum_fusion.7.refs_6_), channel_id=1, source_target_pairs={{0,16},{16,0},{1,17},{17,1},{2,18},{18,2},{3,19},{19,3},{4,20},{20... | collective-permute-start | bytes 1572872 | tf_op jit(solution)/shard_map/ppermute | solution.py:493
  491.1 34.9 %collective-permute-start.127 = (f32[256,256]{1,0:T(8,128)S(1)}, f32[256,256]{1,0:T(8,128)S(1)}, u32[]{:S(2)}, u32[]{:S(2)}) collective-permute-start(f32[256,256]{1,0:T(8,128)S(1)} %broadcast_select_fusion.2), channel_id=1, source_target_pairs={{0,16},{16,0},{1,17},{17,1},{2,18},{18,2},{3,19},{19,3},{4,20},{20... | collective-permute-start | bytes 786440 | tf_op jit(solution)/shard_map/ppermute | solution.py:493
  (260 other events, 2800.6 us)
Sparse Core Ops, SparseCore 0:
  264.8 19.7 reduce-scatter.18
  335.6 18.8 reduce-scatter.16
  357.4 25.3 reduce-scatter.10
  385.1 26.4 reduce-scatter.8
  413.7 26.4 reduce-scatter.22
  442.5 25.9 reduce-scatter.20
  470.8 25.7 reduce-scatter.14
  499.0 25.7 reduce-scatter.12
